TPU v7x, 32 devices: a whole 2x2x4 slice. The times are simulated.
32 devices in a mesh: expert: 16 (over z, y, x), dp: 2 (over core).
Axes of the slice: x: 2, y: 2, z: 4, core: 2. Of those that a mesh axis runs over, the one named last changes fastest.
Arguments:
- expert_ids: int32 [4096, 8], P(('expert', 'dp')), may hold values from 0 to 15, all different within a row; in each aligned block of 128 rows (0 to 127, 128 to 255, ...) at most 80 rows name the same one
- gates: float32 [4096, 8], P(('expert', 'dp')), may hold values from 0.05 to 1
- hidden: bfloat16 [16, 2560, 768], P('expert', 'dp'), may hold values from -6 to 6
- weight: bfloat16 [16, 768, 2048], P('expert'), may hold values from -0.21875 to 0.21875
- out_grad: bfloat16 [4096, 2048], P(('expert', 'dp')), may hold values from -6 to 6
Outputs:
- combined: bfloat16 [4096, 2048], P(('expert', 'dp'))
- gate_grads: float32 [4096, 8], P(('expert', 'dp'))
- hidden_grads: bfloat16 [16, 2560, 768], P('expert', 'dp')
- weight_grads: bfloat16 [16, 768, 2048], P('expert', None, 'dp')
Inputs may be any that keep to these rules, and one draw needn't show every extreme that they name: `expert_ids`: each token names 8 different experts; among the 128 tokens of one device no expert is named more than 80 times, a bound that some block reaches.
All inputs are finite; a program needn't handle non-finite values.
Results may differ from a plain program's by a relative error of at most 0.0049.
Values may be sent and summed in bfloat16 or wider, within the bound.
No kernel may reach another device: no remote copies, remote signals or barrier semaphores. Data moves between devices by JAX's collectives and lax.ppermute only.
A program may use at most 128 MiB of HBM per device.

v0:
```python
import functools

import jax
import jax.numpy as jnp
from jax import lax
from jax.experimental import pallas as pl
from jax.experimental.pallas import tpu as pltpu
from jax.sharding import PartitionSpec as P

F32 = jnp.float32
BF16 = jnp.bfloat16
VMEM_BYTES = 16 * 1024 * 1024
COST = 1024
NEAR_COST = 10**10
LONG_COST = 10**11


def call(body, name, grid, in_specs, out_specs, out_shape, scalars, operands, scratch=(), aliases=None, room=1, cost=COST):
    return pl.pallas_call(
        body,
        name=name,
        grid_spec=pltpu.PrefetchScalarGridSpec(
            num_scalar_prefetch=1, grid=grid, in_specs=in_specs, out_specs=out_specs, scratch_shapes=scratch
        ),
        out_shape=out_shape,
        input_output_aliases=aliases or {},
        cost_estimate=pl.CostEstimate(flops=cost, bytes_accessed=COST, transcendentals=0),
        compiler_params=pltpu.CompilerParams(vmem_limit_bytes=room * VMEM_BYTES),
    )(scalars, *operands)


def direct(body, name, out_shape, scalars, operands, out_specs=None, scratch=(), aliases=None, places=None, room=1, cost=COST):
    places = places or {}
    vmem, smem = pl.BlockSpec(memory_space=pltpu.VMEM), pl.BlockSpec(memory_space=pltpu.SMEM)
    several = isinstance(out_shape, (list, tuple))
    return pl.pallas_call(
        body,
        name=name,
        in_specs=[smem] + [places.get(at, vmem) for at in range(len(operands))],
        out_specs=out_specs or ([vmem] * len(out_shape) if several else vmem),
        out_shape=out_shape,
        scratch_shapes=scratch,
        input_output_aliases=aliases or {},
        cost_estimate=pl.CostEstimate(flops=cost, bytes_accessed=COST, transcendentals=0),
        compiler_params=pltpu.CompilerParams(vmem_limit_bytes=int(room * VMEM_BYTES)),
    )(scalars, *operands)


def follow(value, *earlier):
    anywhere = pl.BlockSpec(memory_space=pl.ANY)
    return pl.pallas_call(
        lambda *refs: None,
        name="follow",
        grid=(1,),
        in_specs=[anywhere] + [pl.BlockSpec((16, 128), lambda i: (0, 0))] * len(earlier),
        out_specs=anywhere,
        out_shape=jax.ShapeDtypeStruct(value.shape, value.dtype),
        input_output_aliases={0: 0},
        cost_estimate=pl.CostEstimate(flops=COST, bytes_accessed=COST, transcendentals=0),
        compiler_params=pltpu.CompilerParams(vmem_limit_bytes=VMEM_BYTES),
    )(value, *earlier)


def token_body(meta, *refs):
    refs[-1][...] = jnp.zeros(refs[-1].shape, F32)


def pieces_of(value):
    high = value.astype(BF16).astype(F32)
    middle = (value - high).astype(BF16).astype(F32)
    return high, middle, value - high - middle


def pack_body(meta, ids, gates, grad, out):
    width, tokens = grad.shape[1], grad.shape[0]
    extent = out.shape[1] - width
    count = meta[6]
    expert = lax.broadcasted_iota(jnp.int32, (extent, tokens), 0)
    piece = jnp.zeros((extent, tokens), jnp.int32)
    for number in range(1, 4):
        piece = piece + jnp.where(expert >= number * count, 1, 0)
    local = expert - piece * count
    named = jnp.zeros((extent, tokens), F32)
    gate = jnp.zeros((extent, tokens), F32)
    for choice in range(ids.shape[0]):
        hit = ids[choice : choice + 1, :] == local
        named = named + jnp.where(hit, 1.0, 0.0)
        gate = gate + jnp.where(hit, gates[choice : choice + 1, :], 0.0)
    before = lax.broadcasted_iota(jnp.int32, (tokens, tokens), 0) < lax.broadcasted_iota(jnp.int32, (tokens, tokens), 1)
    earlier = jnp.dot(named.astype(BF16), jnp.where(before, 1.0, 0.0).astype(BF16), preferred_element_type=F32)
    place = jnp.where(named > 0.0, earlier + meta[2].astype(F32), -1.0)
    high, middle, low = pieces_of(gate)
    table = jnp.where(piece == 0, place, jnp.where(piece == 1, high, jnp.where(piece == 2, middle, low)))
    out[:, :width] = grad[...]
    out[:, width:] = table.T.astype(BF16)


def collect_body(number, count, meta, *refs):
    blocks, outs, table = refs[:number], refs[-3:-1], refs[-1]
    tokens, large = blocks[0].shape[0], outs[0].shape[1]
    strips = ([], [])
    for k in range(number):
        table[...] = blocks[k][:, 2 * large :].astype(F32).T
        for side, out in enumerate(outs):
            start = pl.multiple_of(lax.bitwise_xor(1 - meta[4], side) * large, large)
            out[k * tokens : (k + 1) * tokens, :] = blocks[k][:, pl.ds(start, large)]
            receiver = lax.bitwise_xor(meta[3], 1 << side)
            experts = (receiver, lax.bitwise_xor(receiver, 2 >> side))
            lines = [table[pl.ds(expert + at * count, 1), :] for expert in experts for at in range(4)]
            strips[side].append(jnp.concatenate(lines, 0))
    for strip, out in zip(strips, outs):
        if large > number * tokens:
            strip.append(jnp.zeros((8, large - number * tokens), F32))
        strip = jnp.concatenate(strip, 1)
        out[number * tokens :, :] = jnp.concatenate([strip, jnp.zeros(strip.shape, F32)], 0).astype(BF16)


def forward_body(meta, hidden, weight, out):
    rows = hidden[:, 0].reshape(out.shape[0], hidden.shape[3])
    out[...] = jnp.dot(rows, weight[...], preferred_element_type=F32).astype(BF16)


def forward_first_body(peers, meta, hidden, weight, *refs):
    outs, (rows, matrix, store, sems, out_sems) = refs[: len(peers)], refs[len(peers) :]
    tile = matrix.shape[2]
    copies = []
    for at, peer in enumerate(peers):
        part = hidden.at[:, lax.bitwise_xor(lax.bitwise_and(meta[0], 3), peer)]
        copies.append(pltpu.make_async_copy(part, rows.at[at], sems.at[at]))
    for at in range(matrix.shape[0]):
        part = weight.at[:, at * tile : (at + 1) * tile]
        copies.append(pltpu.make_async_copy(part, matrix.at[at], sems.at[len(peers) + at]))
    for copy in copies:
        copy.start()
    for copy in copies[: len(peers)]:
        copy.wait()
    length = outs[0].shape[0]
    value = rows[...].reshape(len(peers) * length, rows.shape[3])
    results = []
    for at in range(matrix.shape[0]):
        copies[len(peers) + at].wait()
        product = jnp.dot(value, matrix[at], preferred_element_type=F32).astype(BF16)
        for number, out in enumerate(outs):
            store[at, number] = product[number * length : (number + 1) * length]
            target = out.at[:, at * tile : (at + 1) * tile]
            results.append(pltpu.make_async_copy(store.at[at, number], target, out_sems.at[at, number]))
            results[-1].start()
    for copy in results:
        copy.wait()


def turn_body(meta, hidden, after, out, final, final_turned):
    value = hidden[:, 0].reshape(final.shape)
    out[0] = value.T
    final[...] = value
    final_turned[...] = value.T


def turn_other_body(meta, hidden, out):
    out[...] = hidden[...].T


def selection(table, count, expert, rows):
    lines = [table[pl.ds(expert + at * count, 1), :] for at in range(4)]
    return selection_of(lines, rows)


def selection_of(lines, rows):
    place, gate = lines[0], lines[1] + lines[2] + lines[3]
    row = lax.broadcasted_iota(jnp.int32, (rows, place.shape[1]), 0).astype(F32)
    return row == place, gate


def grad_rows_body(plan, jobs, count, groups, meta, *refs):
    number = jobs * groups
    tables, tokens, outs, table = refs[:number], refs[number : 2 * number], refs[-1 - len(plan) : -1], refs[-1]
    rows = outs[0].shape[0] // len(plan[0][1]) // groups
    for job in range(jobs):
        asked = [(out, peer, parts.index(job)) for out, (peer, parts) in zip(outs, plan) if job in parts]
        for group in range(groups):
            table[...] = tables[job * groups + group][...].astype(F32).T
            choices, row_gates = [], []
            for _, peer, _ in asked:
                match, gate = selection(table, count, lax.bitwise_xor(meta[3], peer), rows)
                choices.append(jnp.where(match, 1.0, 0.0))
                row_gates.append(jnp.sum(jnp.where(match, gate, 0.0), 1, keepdims=True))
            choice = jnp.concatenate(choices, 0).astype(BF16)
            picked = jnp.dot(choice, tokens[job * groups + group][...], preferred_element_type=F32)
            value = (picked * jnp.concatenate(row_gates, 0)).astype(BF16)
            place = pl.multiple_of(lax.bitwise_xor(meta[1], group) * rows, rows)
            for at, (out, _, part) in enumerate(asked):
                out[pl.ds(place + part * groups * rows, rows), :] = value[at * rows : (at + 1) * rows]


def direct_rows_body(plan, jobs, number, count, meta, *refs):
    arrays, outs, table = refs[:number], refs[-1 - len(plan) : -1], refs[-1]
    tokens = table.shape[1]
    large = outs[0].shape[1]
    rows = outs[0].shape[0] // len(plan[0][1]) // len(jobs[0])
    for job, sources in enumerate(jobs):
        asked = [(out, peer, parts.index(job)) for out, (peer, parts) in zip(outs, plan) if job in parts]
        for group, (operand, first, whole) in enumerate(sources):
            array, here = arrays[operand], slice(first, first + tokens)
            if whole:
                table[...] = array[here, 2 * large :].astype(F32).T
                columns = pl.ds(pl.multiple_of(lax.bitwise_xor(1 - meta[4], job) * large, large), large)
            else:
                strip = array[array.shape[0] - 16 :, group * tokens : (group + 1) * tokens].astype(F32)
                columns = slice(0, large)
            choices, row_gates = [], []
            for _, peer, _ in asked:
                if whole:
                    match, gate = selection(table, count, lax.bitwise_xor(meta[3], peer), rows)
                else:
                    top = 4 if peer else 0
                    match, gate = selection_of([strip[top + at : top + at + 1] for at in range(4)], rows)
                choices.append(jnp.where(match, 1.0, 0.0))
                row_gates.append(jnp.sum(jnp.where(match, gate, 0.0), 1, keepdims=True))
            choice = jnp.concatenate(choices, 0).astype(BF16)
            picked = jnp.dot(choice, array[here, columns], preferred_element_type=F32)
            value = (picked * jnp.concatenate(row_gates, 0)).astype(BF16)
            place = pl.multiple_of(lax.bitwise_xor(meta[1], group) * rows, rows)
            for at, (out, _, part) in enumerate(asked):
                out[pl.ds(place + part * len(sources) * rows, rows), :] = value[at * rows : (at + 1) * rows]


def direct_combine_body(peers, count, cap, chosen, meta, *refs):
    blocks, returned, (part, table) = refs[: len(chosen)], refs[len(chosen) + 1 : -2], refs[-2:]
    extent, length = table.shape
    width = returned[0].shape[1]
    chunk = min(512, width)
    for number, k in enumerate(chosen):
        here = slice(number * length, (number + 1) * length)
        table[...] = blocks[number][:, width:].astype(F32).T
        start = pl.multiple_of(lax.bitwise_xor(meta[1], k) * cap, cap)
        highs, lows, marks = [], [], []
        for peer in range(peers):
            match, gate = selection(table, count, lax.bitwise_xor(meta[3], peer), cap)
            high = gate.astype(BF16).astype(F32)
            marks.append(jnp.where(match, 1.0, 0.0))
            highs.append(jnp.where(match, high, 0.0))
            lows.append(jnp.where(match, gate - high, 0.0))
        weights = jnp.concatenate([jnp.concatenate(highs, 0).T, jnp.concatenate(lows, 0).T], 0).astype(BF16)
        products = jnp.zeros((peers * cap, length), F32)
        for at in range(0, width, chunk):
            columns = slice(at, at + chunk)
            value = jnp.concatenate([ref[pl.ds(start, cap), columns] for ref in returned], 0)
            total = jnp.dot(weights, value, preferred_element_type=F32)
            part[here, columns] = (total[:length] + total[length:]).astype(part.dtype)
            products = products + lax.dot_general(
                value, blocks[number][:, columns], (((1,), (1,)), ((), ())), preferred_element_type=F32
            )
        products = products * jnp.concatenate(marks, 0)
        inner = [jnp.sum(products[peer * cap : (peer + 1) * cap], 0, keepdims=True) for peer in range(peers)]
        beside = part.shape[1] - width
        row = lax.broadcasted_iota(jnp.int32, (beside, length), 0)
        placed = jnp.zeros((beside, length), F32)
        for peer in range(peers):
            for at, piece in enumerate(pieces_of(inner[peer])):
                placed = jnp.where(row == at * count + lax.bitwise_xor(meta[3], peer), piece, placed)
        part[here, width:] = placed.T.astype(part.dtype)


def combine_body(peers, count, number, meta, *refs):
    packed, tokens, returned = refs[:number], refs[number : 2 * number], refs[2 * number + 1 : 2 * number + 1 + peers]
    part, table, weights, marks, inner = refs[-5:]
    rows, length = returned[0].shape[0], tokens[0].shape[0]
    step, last = pl.program_id(1), pl.num_programs(1) - 1

    def chosen(options):
        value = options[0][...]
        for at in range(1, number):
            value = jnp.where(pl.program_id(0) == at, options[at][...], value)
        return value

    @pl.when(step == 0)
    def _():
        inner[...] = jnp.zeros(inner.shape, F32)
        table[...] = chosen(packed).astype(F32).T
        highs, lows = [], []
        for peer in range(peers):
            match, gate = selection(table, count, lax.bitwise_xor(meta[3], peer), rows)
            high = gate.astype(BF16).astype(F32)
            marks[pl.ds(peer * rows, rows), :] = jnp.where(match, 1.0, 0.0)
            highs.append(jnp.where(match, high, 0.0))
            lows.append(jnp.where(match, gate - high, 0.0))
        weights[:length, :] = jnp.concatenate(highs, 0).T.astype(BF16)
        weights[length:, :] = jnp.concatenate(lows, 0).T.astype(BF16)

    @pl.when(step < last)
    def _():
        value = jnp.concatenate([ref[...] for ref in returned], 0)
        chunk = min(512, value.shape[1])
        for start in range(0, value.shape[1], chunk):
            total = jnp.dot(weights[...], value[:, start : start + chunk], preferred_element_type=F32)
            part[:, start : start + chunk] = (total[:length] + total[length:]).astype(part.dtype)
        products = lax.dot_general(value, chosen(tokens), (((1,), (1,)), ((), ())), preferred_element_type=F32)
        products = products * marks[...]
        for peer in range(peers):
            inner[peer : peer + 1, :] += jnp.sum(products[peer * rows : (peer + 1) * rows], 0, keepdims=True)

    @pl.when(step == last)
    def _():
        extent = -(-3 * count // 128) * 128
        row = lax.broadcasted_iota(jnp.int32, (extent, length), 0)
        placed = jnp.zeros((extent, length), F32)
        for at, piece in enumerate(pieces_of(inner[...])):
            for peer in range(peers):
                place = at * count + lax.bitwise_xor(meta[3], peer)
                placed = jnp.where(row == place, piece[peer : peer + 1, :], placed)
        part[:, :extent] = placed.T.astype(part.dtype)


def send_inside(plan, meta, weight, rows, out, store, sems):
    shape = store.shape[1:]
    length, large = shape[0] * shape[1], weight.shape[1] // 2
    contract = (((1,), (1,)), ((), ()))
    copies = []
    for at, (peer, parts) in enumerate(plan):
        value = jnp.zeros((length, weight.shape[0]), F32)
        for half, (operand, start) in enumerate(parts):
            columns = pl.ds(pl.multiple_of(lax.bitwise_xor(1 - meta[4], half) * large, large), large)
            part = rows[operand][start : start + length, :]
            value = value + lax.dot_general(part, weight[:, columns], contract, preferred_element_type=F32)
        store[at] = value.astype(BF16).reshape(shape)
        copies.append(pltpu.make_async_copy(store.at[at], out.at[:, lax.bitwise_xor(meta[0], peer)], sems.at[at]))
        copies[-1].start()
    return copies


def inside_body(plan, meta, weight, *refs):
    number = 1 + max(at for _, parts in plan for at, _ in parts)
    out, token, store, sems = refs[-4:]
    copies = send_inside(plan, meta, weight, refs[:number], out, store, sems)
    token[...] = jnp.zeros(token.shape, F32)
    for copy in copies:
        copy.wait()


def tail_body(plan, count, meta, weight, *refs):
    number = 1 + max(at for _, parts in plan for at, _ in parts)
    ids, kept, arrived, turned, earlier = refs[number : number + 5]
    out, combined, gate_grads, total, store, sums, sems, sum_sems = refs[-8:]
    copies = send_inside(plan, meta, weight, refs[:number], out, store, sems)
    width, part = combined.shape[1], sums.shape[2]
    for at in range(sums.shape[0]):
        columns = slice(at * part, (at + 1) * part)
        sums[at] = (kept[:, columns] + arrived[:, columns].astype(F32)).astype(BF16)
        copies.append(pltpu.make_async_copy(sums.at[at], combined.at[:, columns], sum_sems.at[at]))
        copies[-1].start()
    pieces = (kept[:, width:] + arrived[:, width:].astype(F32)).T
    inner = pieces[:count] + pieces[count : 2 * count] + pieces[2 * count : 3 * count]
    named = ids[...]
    found = jnp.zeros(gate_grads.shape, F32)
    for expert in range(count):
        found = found + jnp.where(named == expert, inner[expert : expert + 1, :], 0.0)
    gate_grads[...] = found
    operand, start = plan[0][1][1]
    chunk = min(512, total.shape[1])
    for at in range(0, total.shape[1], chunk):
        columns = slice(at, at + chunk)
        part = refs[operand][start : start + turned.shape[1], columns]
        total[:, columns] = jnp.dot(turned[...], part, preferred_element_type=F32) + earlier[:, columns]
    for copy in copies:
        copy.wait()


def weight_grad_body(plan, number, has_earlier, half, meta, turned, *refs):
    rows, (other, own, token) = refs[:number], refs[-3:]
    length, tile = turned.shape[2], own.shape[1] // half
    for side, out in enumerate((other, own)):
        for at in range(half):
            columns = slice(at * tile, (at + 1) * tile)
            value = refs[number + side][:, columns] if has_earlier else jnp.zeros((turned.shape[1], tile), F32)
            for peer, parts in plan:
                operand, start = parts[side]
                part = rows[operand][start : start + length, columns]
                value = value + jnp.dot(turned[peer], part, preferred_element_type=F32)
            out[:, columns] = value.astype(out.dtype)
    token[...] = jnp.zeros(token.shape, F32)


def last_body(parts, meta, turned, rows, earlier, earlier_other, grads, store, sems):
    tile = store.shape[2]
    copies = []
    for at in range(parts):
        columns = slice(at * tile, (at + 1) * tile)
        value = jnp.dot(turned[...], rows[:, columns], preferred_element_type=F32)
        store[at] = (value + earlier[:, columns] + earlier_other[:, columns].astype(F32)).astype(BF16)
        copies.append(pltpu.make_async_copy(store.at[at], grads.at[:, columns], sems.at[at]))
        copies[-1].start()
    for copy in copies:
        copy.wait()


def per_device(expert_ids, gates, hidden, weight, out_grad):
    count = lax.axis_size("expert")
    peers = 1 << ((count.bit_length() - 1) // 2)
    planes = count // peers
    tokens, top = expert_ids.shape
    cap = hidden.shape[1] // count
    width, inside = out_grad.shape[1], hidden.shape[2]
    fold = 1
    while fold * cap % 16:
        fold *= 2
    groups = planes // fold
    group_rows, group_tokens = fold * cap, fold * tokens
    rows = planes * cap
    tile = min(512, width // 2)
    steps = width // tile
    half = steps // 2
    large = width // 2
    room = 1 if fold == 1 else 3
    last = peers - 1
    anywhere = pl.BlockSpec(memory_space=pl.ANY)
    glance = pl.BlockSpec((16, 128), lambda *i: (0, 0))

    me = lax.axis_index("expert")
    core = lax.axis_index("dp")
    column, plane = me % peers, me // peers
    meta = jnp.stack([column, plane // fold, (plane % fold) * cap, me, core, plane, count]).astype(jnp.int32)

    def swap(value, distance):
        return lax.ppermute(value, "expert", [(e, e ^ distance) for e in range(count)])

    def exchange(value):
        return lax.ppermute(value, "dp", [(0, 1), (1, 0)])

    matrix = weight[0]
    if fold == 1:
        blocks = hidden.reshape(planes, peers, cap, inside)
    else:
        blocks = hidden.reshape(planes, peers, cap, inside).transpose(1, 0, 2, 3).reshape(1, peers, rows, inside)
    block = (blocks.shape[0], 1, blocks.shape[2], inside)

    ids_turned = expert_ids.T
    extent = -(-4 * count // 128) * 128
    short = pl.BlockSpec((top, tokens), lambda i, m: (0, 0))
    relay = peers == 4 and fold == 1 and planes * tokens <= large
    packed = call(
        pack_body, "pack", (1,),
        [short, short, pl.BlockSpec((tokens, width), lambda i, m: (0, 0))],
        pl.BlockSpec((tokens, width + extent), lambda i, m: (0, 0)),
        jax.ShapeDtypeStruct((tokens, width + extent), BF16),
        meta, (ids_turned, gates.T, out_grad),
        room=room,
    )
    gathered = [packed]
    for k in range(1, planes):
        if k & (k - 1) == 0:
            gathered.append(swap(packed, peers * k))
        else:
            gathered.append(None)

    def forward(peer, after):
        return call(
            lambda meta, *refs: forward_body(meta, refs[0], refs[1], refs[-1]), f"forward{peer}", (steps,),
            [
                pl.BlockSpec(block, lambda i, m: (0, lax.bitwise_xor(m[0], peer), 0, 0)),
                pl.BlockSpec((inside, tile), lambda i, m: (0, i)),
            ]
            + [glance] * len(after),
            pl.BlockSpec((rows, tile), lambda i, m: (0, i)),
            jax.ShapeDtypeStruct((rows, width), BF16),
            meta, (blocks, matrix, *after),
        )

    outputs, after = {}, ()
    if relay:
        outputs[1], outputs[2] = direct(
            functools.partial(forward_first_body, (1, 2)), "forward1", [jax.ShapeDtypeStruct((rows, width), BF16)] * 2,
            me.astype(jnp.int32).reshape(1), (blocks, matrix),
            scratch=[
                pltpu.VMEM((2, planes, cap, inside), BF16),
                pltpu.VMEM((steps, inside, tile), BF16),
                pltpu.VMEM((steps, 2, rows, tile), BF16),
                pltpu.SemaphoreType.DMA((2 + steps,)),
                pltpu.SemaphoreType.DMA((steps, 2)),
            ],
            out_specs=[anywhere, anywhere],
            places={0: anywhere, 1: anywhere}, room=3.75,
        )
        after = (outputs[2], packed)
    for peer in [peer for peer in list(range(1, peers)) + [0] if peer not in outputs]:
        outputs[peer] = forward(peer, after)
        after = (outputs[peer], packed)
    returned = [outputs[0]] + [swap(outputs[peer], peer) for peer in range(1, peers)]
    turned, hidden_last, turned_last = call(
        turn_body, "turn", (peers,),
        [pl.BlockSpec(block, lambda i, m: (0, lax.bitwise_xor(m[0], i), 0, 0)), glance],
        [pl.BlockSpec((1, inside, rows), lambda i, m: (i, 0, 0)), pl.BlockSpec((rows, inside), lambda i, m: (0, 0)),
         pl.BlockSpec((inside, rows), lambda i, m: (0, 0))],
        [
            jax.ShapeDtypeStruct((peers, inside, rows), BF16), jax.ShapeDtypeStruct((rows, inside), BF16),
            jax.ShapeDtypeStruct((inside, rows), BF16),
        ],
        meta, (blocks, outputs[0]),
    )

    turned_other = call(
        turn_other_body, "turn_other", (1,),
        [pl.BlockSpec((rows, inside), lambda i, m: (0, 0))],
        pl.BlockSpec((inside, rows), lambda i, m: (0, 0)),
        jax.ShapeDtypeStruct((inside, rows), BF16),
        meta, (exchange(hidden_last),),
    )
    for k in range(1, planes):
        lowest = k & -k
        if k != lowest:
            gathered[k] = swap(gathered[k ^ lowest], peers * lowest)
    if fold > 1:
        gathered = [jnp.concatenate(gathered[g * fold : (g + 1) * fold], 0) for g in range(groups)]

    def other_half(i, m):
        return (0, 1 - m[4])

    def own_half(i, m):
        return (0, m[4])

    def build_rows(name, plan, jobs, after, cost=COST):
        sources = [source for job in jobs for source in job]
        return call(
            functools.partial(grad_rows_body, plan, len(jobs), count, groups), name, (1,),
            [pl.BlockSpec((group_tokens, extent), table_at) for _, table_at, _ in sources]
            + [pl.BlockSpec((group_tokens, large), data_at) for _, _, data_at in sources]
            + [glance] * len(after),
            [pl.BlockSpec((len(parts) * rows, large), lambda i, m: (0, 0)) for _, parts in plan],
            [jax.ShapeDtypeStruct((len(parts) * rows, large), BF16) for _, parts in plan],
            meta, (*[value for value, _, _ in sources] * 2, *after),
            scratch=[pltpu.VMEM((extent, group_tokens), F32)],
            room=room, cost=cost,
        )

    def beside(i, m):
        return (0, width // extent)

    jobs = [[(value, beside, at) for value in gathered] for at in (other_half, own_half)]
    if relay:
        plan = ((0, (0, 1)), (1, (1,)), (2, (0,)))
        own_jobs = [[(k, 0, True) for k in range(planes)]] * 2
        made = direct(
            functools.partial(direct_rows_body, plan, own_jobs, planes, count), "own_rows",
            [jax.ShapeDtypeStruct((len(parts) * rows, large), BF16) for _, parts in plan],
            meta, gathered, scratch=[pltpu.VMEM((extent, tokens), F32)],
        )
        beside_shape = jax.ShapeDtypeStruct((planes * tokens + 16, large), BF16)
        collected = direct(
            functools.partial(collect_body, planes, count), "collect", [beside_shape] * 2, meta, gathered,
            scratch=[pltpu.VMEM((extent, tokens), F32)],
        )
        before = (outputs[0], turned_other, made[1], collected[0], *returned[1:last])
        arrival = call(
            token_body, "arrival", (1,), [glance] * len(before), glance, jax.ShapeDtypeStruct((16, 128), F32), meta, before,
        )
        near = [swap(follow(value, arrival, returned[last]), 1 << number) for number, value in enumerate(collected)]
        arrived = [
            [(made[0], 0), (made[0], 1)], [None, (swap(made[1], 1), 0)], [(swap(made[2], 2), 0), None], [None, None],
        ]
    else:
        made = build_rows("own_rows", tuple((peer, (0, 1)) for peer in range(peers)), jobs, (outputs[0],))
        arrived = [[(made[0], 0), (made[0], 1)]]
        for peer in range(1, peers):
            got = swap(made[peer], peer)
            arrived.append([(got, 0), (got, 1)])

    padded = width + -(-3 * count // 128) * 128

    def combine(chosen, dtype, after):
        first, stride = chosen[0], len(chosen) > 1 and chosen[1] - chosen[0]
        columns = width if fold == 1 else large

        def part_of(k, i, m):
            return (lax.bitwise_xor(m[1], k * stride + first), jnp.minimum(i, width // columns - 1))

        blocks_of = [gathered[group] for group in chosen]
        return call(
            functools.partial(combine_body, peers, count, len(chosen)), f"combine{first}", (len(chosen), width // columns + 1),
            [pl.BlockSpec((group_tokens, extent), lambda k, i, m: (0, width // extent))] * len(chosen)
            + [pl.BlockSpec((group_tokens, columns), lambda k, i, m: (0, jnp.minimum(i, width // columns - 1)))] * len(chosen)
            + [glance]
            + [pl.BlockSpec((group_rows, columns), part_of)] * peers,
            pl.BlockSpec((group_tokens, columns), lambda k, i, m: (k, i)),
            jax.ShapeDtypeStruct((len(chosen) * group_tokens, padded), dtype),
            meta, (*blocks_of, *blocks_of, after, *returned),
            scratch=[
                pltpu.VMEM((extent, group_tokens), F32),
                pltpu.VMEM((2 * group_tokens, peers * group_rows), BF16),
                pltpu.VMEM((peers * group_rows, group_tokens), F32),
                pltpu.VMEM((peers, group_tokens), F32),
            ],
            room=room,
        )

    def direct_combine(chosen, dtype, after):
        return direct(
            functools.partial(direct_combine_body, peers, count, cap, tuple(chosen)), f"combine{chosen[0]}",
            jax.ShapeDtypeStruct((len(chosen) * tokens, padded), dtype),
            meta, (*[gathered[k] for k in chosen], after, *returned),
            scratch=[pltpu.VMEM((extent, tokens), F32)],
        )

    if relay:
        combine = direct_combine
    if fold == 1:
        leaving = combine(range(1, planes, 2), BF16, made[0])
        combine_done = combine(range(0, planes, 2), F32, leaving)
        sums = [combine_done[k * tokens : (k + 1) * tokens] for k in range(planes // 2)]
    else:
        parts = [combine([group], F32, made[0]) for group in range(groups)]
        combine_done = parts[-1]
        sums = [parts[k // fold][k % fold * tokens : (k % fold + 1) * tokens] for k in range(planes)]
        leaving = jnp.concatenate(sums[1::2], 0).astype(BF16)
        sums = sums[0::2]
    distance = 1
    first_sums = None
    while len(sums) > 1:
        got = swap(leaving, peers * distance)
        pieces = [got[k * tokens : (k + 1) * tokens].astype(F32) for k in range(len(sums))]
        sums = [mine + piece for mine, piece in zip(sums, pieces)]
        leaving = [value.astype(BF16) for value in sums[1::2]]
        leaving = leaving[0] if len(leaving) == 1 else jnp.concatenate(leaving, 0)
        sums = sums[0::2]
        first_sums = leaving if first_sums is None else first_sums
        distance *= 2
    summed = swap(leaving, peers * distance)

    grads_shape = jax.ShapeDtypeStruct(blocks.shape, BF16)
    def rows_of(chosen):
        arrays, plan = [], []
        for peer in chosen:
            parts = []
            for value, at in arrived[peer]:
                known = [number for number, array in enumerate(arrays) if array is value]
                if not known:
                    arrays.append(value)
                parts.append((known[0] if known else len(arrays) - 1, at * rows))
            plan.append((peer, tuple(parts)))
        return arrays, tuple(plan)

    def inside_grad(chosen, earlier, after):
        arrays, plan = rows_of(chosen)
        operands = [matrix, *arrays, *after] + ([] if earlier is None else [earlier])
        return direct(
            functools.partial(inside_body, plan), f"inside{chosen[0]}",
            [grads_shape, jax.ShapeDtypeStruct((16, 128), F32)],
            meta, operands,
            out_specs=[anywhere, pl.BlockSpec(memory_space=pltpu.VMEM)],
            scratch=[
                pltpu.VMEM((len(chosen), block[0], block[2], inside), BF16),
                pltpu.SemaphoreType.DMA((len(chosen),)),
            ],
            aliases=None if earlier is None else {len(operands): 0},
            places={} if earlier is None else {len(operands) - 1: anywhere},
        )

    def weight_grad(chosen, earlier, after, kind):
        arrays, plan = rows_of(chosen)
        shape = (inside, large)
        return direct(
            functools.partial(weight_grad_body, plan, len(arrays), bool(earlier), half), f"weight_grad{chosen[0]}",
            [jax.ShapeDtypeStruct(shape, kind), jax.ShapeDtypeStruct(shape, F32), jax.ShapeDtypeStruct((16, 128), F32)],
            meta, (turned, *arrays, *earlier, *after),
        )

    hidden_grads, token = inside_grad([0], None, ())
    total_other, total_own, own_token = weight_grad([0], (), (token,), F32)

    if relay:
        plan = ((0, (0,)), (2, (0,)), (0, (1,)), (1, (1,)))
        near_jobs = [[(job, k * tokens, False) for k in range(planes)] for job in range(2)]
        made = direct(
            functools.partial(direct_rows_body, plan, near_jobs, 2, count), "near_rows",
            [jax.ShapeDtypeStruct((rows, large), BF16)] * 4,
            meta, (*near, combine_done, own_token), scratch=[pltpu.VMEM((extent, tokens), F32)], cost=NEAR_COST,
        )
        arrived[1][0], arrived[2][1] = (made[0], 0), (made[2], 0)
        arrived[3] = [(swap(made[1], 2), 0), (swap(made[3], 1), 0)]

    hidden_grads, token = inside_grad(range(1, last), hidden_grads, (made[1][:16, :128], first_sums[:16, :128]))
    total_other, total_own, _ = weight_grad(range(1, last), (total_other, total_own), (token,), BF16)
    total_other = exchange(total_other)
    last_other, _ = arrived[last]
    rows_other = last_other[0] if relay else last_other[0][:rows]

    rows_other = exchange(rows_other)
    arrays, plan = rows_of([last])
    vmem = pl.BlockSpec(memory_space=pltpu.VMEM)
    hidden_grads, combined, gate_grads, total_own = direct(
        functools.partial(tail_body, plan, count), "tail",
        [
            grads_shape, jax.ShapeDtypeStruct((tokens, width), BF16), jax.ShapeDtypeStruct((top, tokens), F32),
            jax.ShapeDtypeStruct((inside, large), F32),
        ],
        meta, (matrix, *arrays, ids_turned, sums[0], summed, turned_last, total_own, hidden_grads),
        out_specs=[anywhere, anywhere, vmem, vmem],
        scratch=[
            pltpu.VMEM((1, block[0], block[2], inside), BF16), pltpu.VMEM((2, tokens, large), BF16),
            pltpu.SemaphoreType.DMA((1,)), pltpu.SemaphoreType.DMA((2,)),
        ],
        aliases={len(arrays) + 7: 0}, places={len(arrays) + 6: anywhere}, cost=LONG_COST,
    )
    weight_grads = direct(
        functools.partial(last_body, 2 * half), "last", jax.ShapeDtypeStruct((inside, large), BF16),
        meta, (turned_other, rows_other, total_own, total_other),
        out_specs=anywhere,
        scratch=[pltpu.VMEM((2 * half, inside, tile // 2), BF16), pltpu.SemaphoreType.DMA((2 * half,))],
    )

    if fold > 1:
        hidden_grads = hidden_grads.reshape(peers, planes, cap, inside).transpose(1, 0, 2, 3)
    return combined, gate_grads.T, hidden_grads.reshape(hidden.shape), weight_grads[None]


def solution(mesh):
    placed = (
        P(("expert", "dp"), None),
        P(("expert", "dp"), None),
        P("expert", "dp", None),
        P("expert", None, None),
        P(("expert", "dp"), None),
    )
    return jax.shard_map(
        per_device,
        mesh=mesh,
        in_specs=placed,
        out_specs=(
            P(("expert", "dp"), None),
            P(("expert", "dp"), None),
            P("expert", "dp", None),
            P("expert", None, "dp"),
        ),
        check_vma=False,
    )
```

profile of v0, /device:TPU:1, one launch (start us, length us, event | category | flops | bytes accessed | tf_op | source)
XLA Modules:
  0.0 132.2 jit_solution(2824482943679040416)
XLA Ops:
  0.7 5.2 %forward1.1 = (bf16[320,2048]{1,0:T(8,128)(2,1)}, bf16[320,2048]{1,0:T(8,128)(2,1)}) custom-call(s32[1]{0:T(128)} %bitcast.2.meta, bf16[4,4,80,768]{3,2,1,0:T(8,128)(2,1)} %bitcast.17, bf16[768,2048]{1,0:T(8,128)(2,1)} %bitcast.11), custom_call_target="tpu_custom_call" | custom-call | flops 1024 | bytes 1024 | tf_op jit(solution)/shard_map/forward1/pallas_call | solution.py:36
  5.8 2.1 %collective-permute-start.4 = (bf16[320,2048]{1,0:T(8,128)(2,1)}, bf16[320,2048]{1,0:T(8,128)(2,1)}, u32[]{:S(2)}, u32[]{:S(2)}) collective-permute-start(bf16[320,2048]{1,0:T(8,128)(2,1)} %get-tuple-element.35), channel_id=1, source_target_pairs={{0,2},{2,0},{4,6},{6,4},{8,10},{10,8},{12,14},{14,12},{16,18},{18,... | collective-permute-start | bytes 3932168 | tf_op jit(solution)/shard_map/ppermute | solution.py:424
  11.2 1.5 %copy-done.1 = bf16[1,1280,768]{2,1,0:T(8,128)(2,1)S(1)} copy-done((bf16[1,1280,768]{2,1,0:T(8,128)(2,1)S(1)}, bf16[1,1280,768]{2,1,0:T(8,128)(2,1)}, u32[]{:S(2)}) %copy-start.1) | copy-done | bytes 1966104
  14.0 2.6 %forward3.1.refs_2_ = bf16[320,2048]{1,0:T(8,128)(2,1)S(1)} custom-call(s32[7]{0:T(128)S(1)} %stack.21.meta, bf16[4,4,80,768]{3,2,1,0:T(8,128)(2,1)S(1)} %bitcast.18, bf16[768,2048]{1,0:T(8,128)(2,1)S(1)} %bitcast.12, bf16[320,2048]{1,0:T(8,128)(2,1)S(1)} %copy-done.2, bf16[128,2176]{1,0:T(8,128)(2,1)S(1)} %pack.1.refs_0_.refs_3_), custom_call_target="tpu_custom_call" | custom-call | flops 1024 | bytes 1024 | tf_op jit(solution)/shard_map/forward3/pallas_call | solution.py:19
  16.8 2.5 %collective-permute-start.1 = (bf16[128,2176]{1,0:T(8,128)(2,1)S(1)}, bf16[128,2176]{1,0:T(8,128)(2,1)S(1)}, u32[]{:S(2)}, u32[]{:S(2)}) collective-permute-start(bf16[128,2176]{1,0:T(8,128)(2,1)S(1)} %pack.1.refs_0_.refs_3_), channel_id=1, source_target_pairs={{0,16},{2,18},{4,20},{6,22},{8,24},{10,26},{12,28},{14,30},{16,0},... | collective-permute-start | bytes 1671176 | tf_op jit(solution)/shard_map/ppermute | solution.py:424
  19.2 2.6 %forward0.1.after.refs_0_.refs_3_ = bf16[320,2048]{1,0:T(8,128)(2,1)S(1)} custom-call(s32[7]{0:T(128)S(1)} %stack.21.meta, bf16[4,4,80,768]{3,2,1,0:T(8,128)(2,1)S(1)} %bitcast.19, bf16[768,2048]{1,0:T(8,128)(2,1)S(1)} %bitcast.13, bf16[320,2048]{1,0:T(8,128)(2,1)S(1)} %forward3.1.refs_2_, bf16[128,2176]{1,0:T(8,128)(2,1)S(1)} %pack.1.refs_0_.refs_3_), custom_call_target="tpu_custom_call" | custom-call | flops 1024 | bytes 1024 | tf_op jit(solution)/shard_map/forward0/pallas_call | solution.py:19
  21.9 1.8 %turn.1 = (bf16[4,768,320]{2,1,0:T(8,128)(2,1)S(1)}, bf16[320,768]{1,0:T(8,128)(2,1)S(1)}, bf16[768,320]{1,0:T(8,128)(2,1)S(1)}) custom-call(s32[7]{0:T(128)S(1)} %stack.21.meta, bf16[4,4,80,768]{3,2,1,0:T(8,128)(2,1)S(1)} %bitcast.20, bf16[320,2048]{1,0:T(8,128)(2,1)S(1)} %forward0.1.after.refs_0_.refs_3_), custom_call_target="tpu_custom_call" | custom-call | flops 1024 | bytes 1024 | tf_op jit(solution)/shard_map/turn/pallas_call | solution.py:19
  23.7 1.9 %collective-permute-start.3 = (bf16[320,768]{1,0:T(8,128)(2,1)S(1)}, bf16[320,768]{1,0:T(8,128)(2,1)S(1)}, u32[]{:S(2)}, u32[]{:S(2)}) collective-permute-start(bf16[320,768]{1,0:T(8,128)(2,1)S(1)} %get-tuple-element.33), channel_id=1, source_target_pairs={{0,1},{1,0},{2,3},{3,2},{4,5},{5,4},{6,7},{7,6},{8,9},{9,8},{10,11... | collective-permute-start | bytes 1474568 | tf_op jit(solution)/shard_map/ppermute | solution.py:427
  25.6 1.5 %collective-permute-done.3.hidden = bf16[320,768]{1,0:T(8,128)(2,1)S(1)} collective-permute-done((bf16[320,768]{1,0:T(8,128)(2,1)S(1)}, bf16[320,768]{1,0:T(8,128)(2,1)S(1)}, u32[]{:S(2)}, u32[]{:S(2)}) %collective-permute-start.3) | collective-permute-done | bytes 491552 | tf_op jit(solution)/shard_map/ppermute | solution.py:427
  28.4 14.8 %collective-permute-done.1.refs_2_.refs_1_ = bf16[128,2176]{1,0:T(8,128)(2,1)S(1)} collective-permute-done((bf16[128,2176]{1,0:T(8,128)(2,1)S(1)}, bf16[128,2176]{1,0:T(8,128)(2,1)S(1)}, u32[]{:S(2)}, u32[]{:S(2)}) %collective-permute-start.1) | collective-permute-done | bytes 557088 | tf_op jit(solution)/shard_map/ppermute | solution.py:424
  43.2 1.6 %collective-permute-start.2 = (bf16[128,2176]{1,0:T(8,128)(2,1)S(1)}, bf16[128,2176]{1,0:T(8,128)(2,1)S(1)}, u32[]{:S(2)}, u32[]{:S(2)}) collective-permute-start(bf16[128,2176]{1,0:T(8,128)(2,1)S(1)} %collective-permute-done.1.refs_2_.refs_1_), channel_id=1, source_target_pairs={{0,8},{2,10},{4,12},{6,14},{8,0},{10,2},{12,4},{14,6},{16,24},{18,... | collective-permute-start | bytes 1671176 | tf_op jit(solution)/shard_map/ppermute | solution.py:424
  45.5 6.3 %collective-permute-done.refs_1_.refs_0_ = bf16[128,2176]{1,0:T(8,128)(2,1)S(1)} collective-permute-done((bf16[128,2176]{1,0:T(8,128)(2,1)S(1)}, bf16[128,2176]{1,0:T(8,128)(2,1)S(1)}, u32[]{:S(2)}, u32[]{:S(2)}) %collective-permute-start) | collective-permute-done | bytes 557088 | tf_op jit(solution)/shard_map/ppermute | solution.py:424
  51.8 11.9 %collective-permute-done.2.refs_3_.refs_1_ = bf16[128,2176]{1,0:T(8,128)(2,1)S(1)} collective-permute-done((bf16[128,2176]{1,0:T(8,128)(2,1)S(1)}, bf16[128,2176]{1,0:T(8,128)(2,1)S(1)}, u32[]{:S(2)}, u32[]{:S(2)}) %collective-permute-start.2) | collective-permute-done | bytes 557088 | tf_op jit(solution)/shard_map/ppermute | solution.py:424
  64.5 1.7 %own_rows.1 = (bf16[640,1024]{1,0:T(8,128)(2,1)S(1)}, bf16[320,1024]{1,0:T(8,128)(2,1)S(1)}, bf16[320,1024]{1,0:T(8,128)(2,1)S(1)}) custom-call(s32[7]{0:T(128)S(1)} %stack.21.meta, bf16[128,2176]{1,0:T(8,128)(2,1)S(1)} %pack.1.refs_0_.refs_3_, bf16[128,2176]{1,0:T(8,128)(2,1)S(1)} %collective-permute-done.refs_1_.refs_0_, ...), custom_call_target="tpu_custom_call" | custom-call | flops 1024 | bytes 1024 | tf_op jit(solution)/shard_map/own_rows/pallas_call | solution.py:36
  68.6 1.3 %collective-permute-start.8 = (bf16[528,1024]{1,0:T(8,128)(2,1)S(1)}, bf16[528,1024]{1,0:T(8,128)(2,1)S(1)}, u32[]{:S(2)}, u32[]{:S(2)}) collective-permute-start(bf16[528,1024]{1,0:T(8,128)(2,1)S(1)} %follow.3), channel_id=1, source_target_pairs={{0,4},{2,6},{4,0},{6,2},{8,12},{10,14},{12,8},{14,10},{16,20},{18,... | collective-permute-start | bytes 3244040 | tf_op jit(solution)/shard_map/ppermute | solution.py:424
  69.9 4.1 %combine1.1.refs_2_ = bf16[256,2176]{1,0:T(8,128)(2,1)S(1)} custom-call(s32[7]{0:T(128)S(1)} %stack.21.meta, bf16[128,2176]{1,0:T(8,128)(2,1)S(1)} %collective-permute-done.refs_1_.refs_0_, bf16[128,2176]{1,0:T(8,128)(2,1)S(1)} %collective-permute-done.2.refs_3_.refs_1_, bf16[640,1024]{1,0:T(8,128)(2,1)S(1)} %get-tuple-element.37.refs_2_.refs_0_, ...), custom_call_target="tpu_custom_call" | custom-call | flops 1024 | bytes 1024 | tf_op jit(solution)/shard_map/combine1/pallas_call | solution.py:36
  74.4 2.6 %inside0.1 = (bf16[4,4,80,768]{3,2,1,0:T(8,128)(2,1)}, f32[16,128]{1,0:T(8,128)S(1)}) custom-call(s32[7]{0:T(128)S(1)} %stack.21.meta, bf16[768,2048]{1,0:T(8,128)(2,1)S(1)} %bitcast.14, bf16[640,1024]{1,0:T(8,128)(2,1)S(1)} %get-tuple-element.37.refs_2_.refs_0_), custom_call_target="tpu_custom_call" | custom-call | flops 1024 | bytes 1024 | tf_op jit(solution)/shard_map/inside0/pallas_call | solution.py:36
  77.2 2.3 %weight_grad0.1 = (f32[768,1024]{1,0:T(8,128)S(1)}, f32[768,1024]{1,0:T(8,128)S(1)}, f32[16,128]{1,0:T(8,128)S(1)}) custom-call(s32[7]{0:T(128)S(1)} %stack.21.meta, bf16[4,768,320]{2,1,0:T(8,128)(2,1)S(1)} %get-tuple-element.38.turned, bf16[640,1024]{1,0:T(8,128)(2,1)S(1)} %get-tuple-element.37.refs_2_.refs_0_, f32[16,128]{1,0:T(8,128)S(1)} %get-tuple-element.39.refs_1_), custom_call_target="tpu_custom_call" | custom-call | flops 1024 | bytes 1024 | tf_op jit(solution)/shard_map/weight_grad0/pallas_call | solution.py:36
  79.6 4.1 %combine0.1.refs_2_ = f32[256,2176]{1,0:T(8,128)S(1)} custom-call(s32[7]{0:T(128)S(1)} %stack.21.meta, bf16[128,2176]{1,0:T(8,128)(2,1)S(1)} %pack.1.refs_0_.refs_3_, bf16[128,2176]{1,0:T(8,128)(2,1)S(1)} %collective-permute-done.1.refs_2_.refs_1_, bf16[256,2176]{1,0:T(8,128)(2,1)S(1)} %combine1.1.refs_2_, ...), custom_call_target="tpu_custom_call" | custom-call | flops 1024 | bytes 1024 | tf_op jit(solution)/shard_map/combine0/pallas_call | solution.py:36
  83.7 7.8 %collective-permute-done.7.refs_0_ = bf16[528,1024]{1,0:T(8,128)(2,1)S(1)} collective-permute-done((bf16[528,1024]{1,0:T(8,128)(2,1)S(1)}, bf16[528,1024]{1,0:T(8,128)(2,1)S(1)}, u32[]{:S(2)}, u32[]{:S(2)}) %collective-permute-start.7) | collective-permute-done | bytes 1081376 | tf_op jit(solution)/shard_map/ppermute | solution.py:424
  92.4 1.4 %near_rows.1 = (bf16[320,1024]{1,0:T(8,128)(2,1)S(1)}, bf16[320,1024]{1,0:T(8,128)(2,1)S(1)}, bf16[320,1024]{1,0:T(8,128)(2,1)S(1)}, bf16[320,1024]{1,0:T(8,128)(2,1)S(1)}) custom-call(s32[7]{0:T(128)S(1)} %stack.21.meta, bf16[528,1024]{1,0:T(8,128)(2,1)S(1)} %collective-permute-done.7.refs_0_, bf16[528,1024]{1,0:T(8,128)(2,1)S(1)} %collective-permute-done.8.refs_1_, ...), custom_call_target="tpu_custom_call" | custom-call | flops 10000000000 | bytes 1024 | tf_op jit(solution)/shard_map/near_rows/pallas_call | solution.py:36
  94.2 1.4 %collective-permute-start.9 = (bf16[320,1024]{1,0:T(8,128)(2,1)S(1)}, bf16[320,1024]{1,0:T(8,128)(2,1)S(1)}, u32[]{:S(2)}, u32[]{:S(2)}) collective-permute-start(bf16[320,1024]{1,0:T(8,128)(2,1)S(1)} %get-tuple-element.41), channel_id=1, source_target_pairs={{0,4},{2,6},{4,0},{6,2},{8,12},{10,14},{12,8},{14,10},{16,20},{18,... | collective-permute-start | bytes 1966088 | tf_op jit(solution)/shard_map/ppermute | solution.py:424
  95.7 2.8 %collective-permute-done.11 = bf16[256,2176]{1,0:T(8,128)(2,1)S(1)} collective-permute-done((bf16[256,2176]{1,0:T(8,128)(2,1)S(1)}, bf16[256,2176]{1,0:T(8,128)(2,1)S(1)}, u32[]{:S(2)}, u32[]{:S(2)}) %collective-permute-start.11) | collective-permute-done | bytes 1114144 | tf_op jit(solution)/shard_map/ppermute | solution.py:424
  99.0 7.5 %collective-permute-done.14.refs_2_ = bf16[320,1024]{1,0:T(8,128)(2,1)S(1)} collective-permute-done((bf16[320,1024]{1,0:T(8,128)(2,1)S(1)}, bf16[320,1024]{1,0:T(8,128)(2,1)S(1)}, u32[]{:S(2)}, u32[]{:S(2)}) %collective-permute-start.14) | collective-permute-done | bytes 655392 | tf_op jit(solution)/shard_map/ppermute | solution.py:424
  106.5 3.6 %inside1.1 = (bf16[4,4,80,768]{3,2,1,0:T(8,128)(2,1)}, f32[16,128]{1,0:T(8,128)S(1)}) custom-call(s32[7]{0:T(128)S(1)} %stack.21.meta, bf16[768,2048]{1,0:T(8,128)(2,1)S(1)} %bitcast.15, bf16[320,1024]{1,0:T(8,128)(2,1)S(1)} %get-tuple-element.44.refs_0_, bf16[320,1024]{1,0:T(8,128)(2,1)S(1)} %collective-permute-done.13.refs_1_, ...), custom_call_target="tpu_custom_call", output_to_operand_aliasing={{0}: (8, {})} | custom-call | flops 1024 | bytes 1024 | tf_op jit(solution)/shard_map/inside1/pallas_call | solution.py:36
  110.1 4.7 %weight_grad1.1 = (bf16[768,1024]{1,0:T(8,128)(2,1)S(1)}, f32[768,1024]{1,0:T(8,128)S(1)}, f32[16,128]{1,0:T(8,128)}) custom-call(s32[7]{0:T(128)S(1)} %stack.21.meta, bf16[4,768,320]{2,1,0:T(8,128)(2,1)S(1)} %get-tuple-element.38.turned, bf16[320,1024]{1,0:T(8,128)(2,1)S(1)} %get-tuple-element.44.refs_0_, ...), custom_call_target="tpu_custom_call" | custom-call | flops 1024 | bytes 1024 | tf_op jit(solution)/shard_map/weight_grad1/pallas_call | solution.py:36
  114.8 4.4 %collective-permute-start.16 = (bf16[768,1024]{1,0:T(8,128)(2,1)S(1)}, bf16[768,1024]{1,0:T(8,128)(2,1)S(1)}, u32[]{:S(2)}, u32[]{:S(2)}) collective-permute-start(bf16[768,1024]{1,0:T(8,128)(2,1)S(1)} %get-tuple-element.57), channel_id=1, source_target_pairs={{0,1},{1,0},{2,3},{3,2},{4,5},{5,4},{6,7},{7,6},{8,9},{9,8},{10,11... | collective-permute-start | bytes 4718600 | tf_op jit(solution)/shard_map/ppermute | solution.py:427
  119.2 1.3 %collective-permute-done.9.refs_0_ = bf16[320,1024]{1,0:T(8,128)(2,1)S(1)} collective-permute-done((bf16[320,1024]{1,0:T(8,128)(2,1)S(1)}, bf16[320,1024]{1,0:T(8,128)(2,1)S(1)}, u32[]{:S(2)}, u32[]{:S(2)}) %collective-permute-start.9) | collective-permute-done | bytes 655392 | tf_op jit(solution)/shard_map/ppermute | solution.py:424
  120.5 2.4 %collective-permute-start.15 = (bf16[320,1024]{1,0:T(8,128)(2,1)S(1)}, bf16[320,1024]{1,0:T(8,128)(2,1)S(1)}, u32[]{:S(2)}, u32[]{:S(2)}) collective-permute-start(bf16[320,1024]{1,0:T(8,128)(2,1)S(1)} %collective-permute-done.9.refs_0_), channel_id=1, source_target_pairs={{0,1},{1,0},{2,3},{3,2},{4,5},{5,4},{6,7},{7,6},{8,9},{9,8},{10,11... | collective-permute-start | bytes 1966088 | tf_op jit(solution)/shard_map/ppermute | solution.py:427
  122.9 2.4 %collective-permute-done.12.refs_4_ = bf16[128,2176]{1,0:T(8,128)(2,1)S(1)} collective-permute-done((bf16[128,2176]{1,0:T(8,128)(2,1)S(1)}, bf16[128,2176]{1,0:T(8,128)(2,1)S(1)}, u32[]{:S(2)}, u32[]{:S(2)}) %collective-permute-start.12) | collective-permute-done | bytes 557088 | tf_op jit(solution)/shard_map/ppermute | solution.py:424
  125.4 4.1 %tail.1 = (bf16[4,4,80,768]{3,2,1,0:T(8,128)(2,1)}, bf16[128,2048]{1,0:T(8,128)(2,1)}, f32[8,128]{1,0:T(8,128)}, f32[768,1024]{1,0:T(8,128)S(1)}) custom-call(s32[7]{0:T(128)S(1)} %stack.21.meta, bf16[768,2048]{1,0:T(8,128)(2,1)S(1)} %bitcast.16, bf16[320,1024]{1,0:T(8,128)(2,1)S(1)} %collective-permute-done.9.refs_0_, ...), custom_call_target="tpu_custom_call", output_to_operand_aliasing={{0}: (9, {})} | custom-call | flops 99999997952 | bytes 1024 | tf_op jit(solution)/shard_map/tail/pallas_call | solution.py:36
  129.5 2.5 %last.1 = bf16[768,1024]{1,0:T(8,128)(2,1)} custom-call(s32[7]{0:T(128)S(1)} %stack.21.meta, bf16[768,320]{1,0:T(8,128)(2,1)S(1)} %turn_other.1.refs_1_.turned, bf16[320,1024]{1,0:T(8,128)(2,1)S(1)} %collective-permute-done.15.rows, f32[768,1024]{1,0:T(8,128)S(1)} %get-tuple-element.56.earlier, bf16[768,1024]{1,0:T(8,128)(2,1)S(1)} %collective-permute-done.16.earlier_other), custom_call_target="tpu_custom_call" | custom-call | flops 1024 | bytes 1024 | tf_op jit(solution)/shard_map/last/pallas_call | solution.py:36
  (38 shorter events, 12.4 us)
Async XLA Ops:
  0.6 8.6 %copy-start.4 = (f32[128,8]{0,1:T(8,128)S(1)}, f32[128,8]{0,1:T(8,128)}, u32[]{:S(2)}) copy-start(f32[128,8]{0,1:T(8,128)} %param.6) | copy-start | bytes 12292
  0.6 8.6 %copy-start.5 = (s32[128,8]{0,1:T(8,128)S(1)}, s32[128,8]{0,1:T(8,128)}, u32[]{:S(2)}) copy-start(s32[128,8]{0,1:T(8,128)} %param.5) | copy-start | bytes 12292
  0.7 10.5 %copy-start = (bf16[1,768,2048]{2,1,0:T(8,128)(2,1)S(1)}, bf16[1,768,2048]{2,1,0:T(8,128)(2,1)}, u32[]{:S(2)}) copy-start(bf16[1,768,2048]{2,1,0:T(8,128)(2,1)} %param.8) | copy-start | bytes 9437188
  5.8 60.3 %collective-permute-start.4 = (bf16[320,2048]{1,0:T(8,128)(2,1)}, bf16[320,2048]{1,0:T(8,128)(2,1)}, u32[]{:S(2)}, u32[]{:S(2)}) collective-permute-start(bf16[320,2048]{1,0:T(8,128)(2,1)} %get-tuple-element.35), channel_id=1, source_target_pairs={{0,2},{2,0},{4,6},{6,4},{8,10},{10,8},{12,14},{14,12},{16,18},{18,... | collective-permute-start | bytes 3932168 | tf_op jit(solution)/shard_map/ppermute | solution.py:424
  7.9 58.2 %collective-permute-start.5 = (bf16[320,2048]{1,0:T(8,128)(2,1)}, bf16[320,2048]{1,0:T(8,128)(2,1)}, u32[]{:S(2)}, u32[]{:S(2)}) collective-permute-start(bf16[320,2048]{1,0:T(8,128)(2,1)} %get-tuple-element.32.refs_2_), channel_id=1, source_target_pairs={{0,4},{2,6},{4,0},{6,2},{8,12},{10,14},{12,8},{14,10},{16,20},{18,... | collective-permute-start | bytes 3932168 | tf_op jit(solution)/shard_map/ppermute | solution.py:424
  9.3 1.0 copy-start.3
  11.2 1.5 %copy-start.1 = (bf16[1,1280,768]{2,1,0:T(8,128)(2,1)S(1)}, bf16[1,1280,768]{2,1,0:T(8,128)(2,1)}, u32[]{:S(2)}) copy-start(bf16[1,1280,768]{2,1,0:T(8,128)(2,1)} %param.7) | copy-start | bytes 5898244
  12.7 1.3 copy-start.2
  16.7 50.7 %collective-permute-start.6 = (bf16[320,2048]{1,0:T(8,128)(2,1)S(1)}, bf16[320,2048]{1,0:T(8,128)(2,1)S(1)}, u32[]{:S(2)}, u32[]{:S(2)}) collective-permute-start(bf16[320,2048]{1,0:T(8,128)(2,1)S(1)} %forward3.1.refs_2_), channel_id=1, source_target_pairs={{0,6},{2,4},{4,2},{6,0},{8,14},{10,12},{12,10},{14,8},{16,22},{18,... | collective-permute-start | bytes 3932168 | tf_op jit(solution)/shard_map/ppermute | solution.py:424
  16.8 26.4 %collective-permute-start.1 = (bf16[128,2176]{1,0:T(8,128)(2,1)S(1)}, bf16[128,2176]{1,0:T(8,128)(2,1)S(1)}, u32[]{:S(2)}, u32[]{:S(2)}) collective-permute-start(bf16[128,2176]{1,0:T(8,128)(2,1)S(1)} %pack.1.refs_0_.refs_3_), channel_id=1, source_target_pairs={{0,16},{2,18},{4,20},{6,22},{8,24},{10,26},{12,28},{14,30},{16,0},... | collective-permute-start | bytes 1671176 | tf_op jit(solution)/shard_map/ppermute | solution.py:424
  23.7 3.3 %collective-permute-start.3 = (bf16[320,768]{1,0:T(8,128)(2,1)S(1)}, bf16[320,768]{1,0:T(8,128)(2,1)S(1)}, u32[]{:S(2)}, u32[]{:S(2)}) collective-permute-start(bf16[320,768]{1,0:T(8,128)(2,1)S(1)} %get-tuple-element.33), channel_id=1, source_target_pairs={{0,1},{1,0},{2,3},{3,2},{4,5},{5,4},{6,7},{7,6},{8,9},{9,8},{10,11... | collective-permute-start | bytes 1474568 | tf_op jit(solution)/shard_map/ppermute | solution.py:427
  27.1 24.7 %collective-permute-start = (bf16[128,2176]{1,0:T(8,128)(2,1)S(1)}, bf16[128,2176]{1,0:T(8,128)(2,1)S(1)}, u32[]{:S(2)}, u32[]{:S(2)}) collective-permute-start(bf16[128,2176]{1,0:T(8,128)(2,1)S(1)} %pack.1.refs_0_.refs_3_), channel_id=1, source_target_pairs={{0,8},{2,10},{4,12},{6,14},{8,0},{10,2},{12,4},{14,6},{16,24},{18,... | collective-permute-start | bytes 1671176 | tf_op jit(solution)/shard_map/ppermute | solution.py:424
  43.2 20.6 %collective-permute-start.2 = (bf16[128,2176]{1,0:T(8,128)(2,1)S(1)}, bf16[128,2176]{1,0:T(8,128)(2,1)S(1)}, u32[]{:S(2)}, u32[]{:S(2)}) collective-permute-start(bf16[128,2176]{1,0:T(8,128)(2,1)S(1)} %collective-permute-done.1.refs_2_.refs_1_), channel_id=1, source_target_pairs={{0,8},{2,10},{4,12},{6,14},{8,0},{10,2},{12,4},{14,6},{16,24},{18,... | collective-permute-start | bytes 1671176 | tf_op jit(solution)/shard_map/ppermute | solution.py:424
  67.4 24.0 %collective-permute-start.7 = (bf16[528,1024]{1,0:T(8,128)(2,1)S(1)}, bf16[528,1024]{1,0:T(8,128)(2,1)S(1)}, u32[]{:S(2)}, u32[]{:S(2)}) collective-permute-start(bf16[528,1024]{1,0:T(8,128)(2,1)S(1)} %follow.2), channel_id=1, source_target_pairs={{0,2},{2,0},{4,6},{6,4},{8,10},{10,8},{12,14},{14,12},{16,18},{18,... | collective-permute-start | bytes 3244040 | tf_op jit(solution)/shard_map/ppermute | solution.py:424
  68.6 23.9 %collective-permute-start.8 = (bf16[528,1024]{1,0:T(8,128)(2,1)S(1)}, bf16[528,1024]{1,0:T(8,128)(2,1)S(1)}, u32[]{:S(2)}, u32[]{:S(2)}) collective-permute-start(bf16[528,1024]{1,0:T(8,128)(2,1)S(1)} %follow.3), channel_id=1, source_target_pairs={{0,4},{2,6},{4,0},{6,2},{8,12},{10,14},{12,8},{14,10},{16,20},{18,... | collective-permute-start | bytes 3244040 | tf_op jit(solution)/shard_map/ppermute | solution.py:424
  74.0 24.4 %collective-permute-start.11 = (bf16[256,2176]{1,0:T(8,128)(2,1)S(1)}, bf16[256,2176]{1,0:T(8,128)(2,1)S(1)}, u32[]{:S(2)}, u32[]{:S(2)}) collective-permute-start(bf16[256,2176]{1,0:T(8,128)(2,1)S(1)} %combine1.1.refs_2_), channel_id=1, source_target_pairs={{0,8},{2,10},{4,12},{6,14},{8,0},{10,2},{12,4},{14,6},{16,24},{18,... | collective-permute-start | bytes 3342344 | tf_op jit(solution)/shard_map/ppermute | solution.py:424
  74.1 32.4 %collective-permute-start.13 = (bf16[320,1024]{1,0:T(8,128)(2,1)S(1)}, bf16[320,1024]{1,0:T(8,128)(2,1)S(1)}, u32[]{:S(2)}, u32[]{:S(2)}) collective-permute-start(bf16[320,1024]{1,0:T(8,128)(2,1)S(1)} %get-tuple-element.34.refs_2_), channel_id=1, source_target_pairs={{0,2},{2,0},{4,6},{6,4},{8,10},{10,8},{12,14},{14,12},{16,18},{18,... | collective-permute-start | bytes 1966088 | tf_op jit(solution)/shard_map/ppermute | solution.py:424
  77.0 29.5 %collective-permute-start.14 = (bf16[320,1024]{1,0:T(8,128)(2,1)S(1)}, bf16[320,1024]{1,0:T(8,128)(2,1)S(1)}, u32[]{:S(2)}, u32[]{:S(2)}) collective-permute-start(bf16[320,1024]{1,0:T(8,128)(2,1)S(1)} %get-tuple-element.45), channel_id=1, source_target_pairs={{0,4},{2,6},{4,0},{6,2},{8,12},{10,14},{12,8},{14,10},{16,20},{18,... | collective-permute-start | bytes 1966088 | tf_op jit(solution)/shard_map/ppermute | solution.py:424
  93.9 31.5 %collective-permute-start.10 = (bf16[320,1024]{1,0:T(8,128)(2,1)S(1)}, bf16[320,1024]{1,0:T(8,128)(2,1)S(1)}, u32[]{:S(2)}, u32[]{:S(2)}) collective-permute-start(bf16[320,1024]{1,0:T(8,128)(2,1)S(1)} %get-tuple-element.42), channel_id=1, source_target_pairs={{0,2},{2,0},{4,6},{6,4},{8,10},{10,8},{12,14},{14,12},{16,18},{18,... | collective-permute-start | bytes 1966088 | tf_op jit(solution)/shard_map/ppermute | solution.py:424
  94.2 26.3 %collective-permute-start.9 = (bf16[320,1024]{1,0:T(8,128)(2,1)S(1)}, bf16[320,1024]{1,0:T(8,128)(2,1)S(1)}, u32[]{:S(2)}, u32[]{:S(2)}) collective-permute-start(bf16[320,1024]{1,0:T(8,128)(2,1)S(1)} %get-tuple-element.41), channel_id=1, source_target_pairs={{0,4},{2,6},{4,0},{6,2},{8,12},{10,14},{12,8},{14,10},{16,20},{18,... | collective-permute-start | bytes 1966088 | tf_op jit(solution)/shard_map/ppermute | solution.py:424
  98.6 26.7 %collective-permute-start.12 = (bf16[128,2176]{1,0:T(8,128)(2,1)S(1)}, bf16[128,2176]{1,0:T(8,128)(2,1)S(1)}, u32[]{:S(2)}, u32[]{:S(2)}) collective-permute-start(bf16[128,2176]{1,0:T(8,128)(2,1)S(1)} %get-tuple-element.58), channel_id=1, source_target_pairs={{0,16},{2,18},{4,20},{6,22},{8,24},{10,26},{12,28},{14,30},{16,0},... | collective-permute-start | bytes 1671176 | tf_op jit(solution)/shard_map/ppermute | solution.py:424
  114.8 14.7 %collective-permute-start.16 = (bf16[768,1024]{1,0:T(8,128)(2,1)S(1)}, bf16[768,1024]{1,0:T(8,128)(2,1)S(1)}, u32[]{:S(2)}, u32[]{:S(2)}) collective-permute-start(bf16[768,1024]{1,0:T(8,128)(2,1)S(1)} %get-tuple-element.57), channel_id=1, source_target_pairs={{0,1},{1,0},{2,3},{3,2},{4,5},{5,4},{6,7},{7,6},{8,9},{9,8},{10,11... | collective-permute-start | bytes 4718600 | tf_op jit(solution)/shard_map/ppermute | solution.py:427
  120.5 8.9 %collective-permute-start.15 = (bf16[320,1024]{1,0:T(8,128)(2,1)S(1)}, bf16[320,1024]{1,0:T(8,128)(2,1)S(1)}, u32[]{:S(2)}, u32[]{:S(2)}) collective-permute-start(bf16[320,1024]{1,0:T(8,128)(2,1)S(1)} %collective-permute-done.9.refs_0_), channel_id=1, source_target_pairs={{0,1},{1,0},{2,3},{3,2},{4,5},{5,4},{6,7},{7,6},{8,9},{9,8},{10,11... | collective-permute-start | bytes 1966088 | tf_op jit(solution)/shard_map/ppermute | solution.py:427
where the time goes:
time: 133 us; the launch traced here: 132 us
  waiting for transfers between devices  57.3 us (43%)
  Pallas kernels  46.9 us (35%)
  starting transfers between devices  22.8 us (17%)
  local copies, waits for them, and re-layouts  3.99 us (3%)
    ppermute x14, waiting for transfers between devices, swap(): lax.ppermute(value, 'expert', [(e, e ^ distance) for e in range(count)])  55.8 us
    pallas_call x12, Pallas kernels, direct(): pl.pallas_call(body, name=name, in_specs=[smem] + [places.get(at, vmem) f...  37 us
    ppermute x14, starting transfers between devices, swap(): lax.ppermute(value, 'expert', [(e, e ^ distance) for e in range(count)])  14.1 us
    pallas_call x6, Pallas kernels, call(): pl.pallas_call(body, name=name, grid_spec=pltpu.PrefetchScalarGridSpec(nu...  9.91 us
    ppermute x3, starting transfers between devices, exchange(): return lax.ppermute(value, 'dp', [(0, 1), (1, 0)])  8.66 us
    unnamed x12, local copies, waits for them, and re-layouts  3.91 us
  transfers between devices with their start and end apart: 17, of which 10 were waited for; matrix products, arithmetic and copies ran while one was open for 0% of the time, Pallas kernels for 30%

commit v1 on v0

--- a/solution.py
+++ b/solution.py
@@ -29,7 +29,7 @@
     )(scalars, *operands)
 
 
-def direct(body, name, out_shape, scalars, operands, out_specs=None, scratch=(), aliases=None, places=None, room=1, cost=COST):
+def direct(body, name, out_shape, scalars, operands, out_specs=None, scratch=(), aliases=None, places=None, room=0.5, cost=COST):
     places = places or {}
     vmem, smem = pl.BlockSpec(memory_space=pltpu.VMEM), pl.BlockSpec(memory_space=pltpu.SMEM)
     several = isinstance(out_shape, (list, tuple))

time: 133 us -> 133 us (level)
  no operation moved by 1% of the time
where the time goes in v1:
time: 133 us; the launch traced here: 132 us
  waiting for transfers between devices  57.3 us (43%)
  Pallas kernels  46.9 us (35%)
  starting transfers between devices  22.8 us (17%)
  local copies, waits for them, and re-layouts  3.99 us (3%)
    ppermute x14, waiting for transfers between devices, swap(): lax.ppermute(value, 'expert', [(e, e ^ distance) for e in range(count)])  55.8 us
    pallas_call x12, Pallas kernels, direct(): pl.pallas_call(body, name=name, in_specs=[smem] + [places.get(at, vmem) f...  37 us
    ppermute x14, starting transfers between devices, swap(): lax.ppermute(value, 'expert', [(e, e ^ distance) for e in range(count)])  14.1 us
    pallas_call x6, Pallas kernels, call(): pl.pallas_call(body, name=name, grid_spec=pltpu.PrefetchScalarGridSpec(nu...  9.91 us
    ppermute x3, starting transfers between devices, exchange(): return lax.ppermute(value, 'dp', [(0, 1), (1, 0)])  8.69 us
    unnamed x12, local copies, waits for them, and re-layouts  3.91 us
  transfers between devices with their start and end apart: 17, of which 10 were waited for; matrix products, arithmetic and copies ran while one was open for 0% of the time, Pallas kernels for 30%

profile of v1, /device:TPU:1, one launch (start us, length us, event | category | flops | bytes accessed | tf_op | source)
XLA Modules:
  0.0 132.2 jit_solution(8506345174362947922)
XLA Ops:
  0.7 5.2 %forward1.1 = (bf16[320,2048]{1,0:T(8,128)(2,1)}, bf16[320,2048]{1,0:T(8,128)(2,1)}) custom-call(s32[1]{0:T(128)} %bitcast.2.meta, bf16[4,4,80,768]{3,2,1,0:T(8,128)(2,1)} %bitcast.17, bf16[768,2048]{1,0:T(8,128)(2,1)} %bitcast.11), custom_call_target="tpu_custom_call" | custom-call | flops 1024 | bytes 1024 | tf_op jit(solution)/shard_map/forward1/pallas_call | solution.py:36
  5.8 2.1 %collective-permute-start.4 = (bf16[320,2048]{1,0:T(8,128)(2,1)}, bf16[320,2048]{1,0:T(8,128)(2,1)}, u32[]{:S(2)}, u32[]{:S(2)}) collective-permute-start(bf16[320,2048]{1,0:T(8,128)(2,1)} %get-tuple-element.35), channel_id=1, source_target_pairs={{0,2},{2,0},{4,6},{6,4},{8,10},{10,8},{12,14},{14,12},{16,18},{18,... | collective-permute-start | bytes 3932168 | tf_op jit(solution)/shard_map/ppermute | solution.py:424
  11.2 1.5 %copy-done.1 = bf16[1,1280,768]{2,1,0:T(8,128)(2,1)S(1)} copy-done((bf16[1,1280,768]{2,1,0:T(8,128)(2,1)S(1)}, bf16[1,1280,768]{2,1,0:T(8,128)(2,1)}, u32[]{:S(2)}) %copy-start.1) | copy-done | bytes 1966104
  12.7 1.3 copy-done.2
  14.0 2.6 %forward3.1.refs_2_ = bf16[320,2048]{1,0:T(8,128)(2,1)S(1)} custom-call(s32[7]{0:T(128)S(1)} %stack.21.meta, bf16[4,4,80,768]{3,2,1,0:T(8,128)(2,1)S(1)} %bitcast.18, bf16[768,2048]{1,0:T(8,128)(2,1)S(1)} %bitcast.12, bf16[320,2048]{1,0:T(8,128)(2,1)S(1)} %copy-done.2, bf16[128,2176]{1,0:T(8,128)(2,1)S(1)} %pack.1.refs_0_.refs_3_), custom_call_target="tpu_custom_call" | custom-call | flops 1024 | bytes 1024 | tf_op jit(solution)/shard_map/forward3/pallas_call | solution.py:19
  16.8 2.5 %collective-permute-start.1 = (bf16[128,2176]{1,0:T(8,128)(2,1)S(1)}, bf16[128,2176]{1,0:T(8,128)(2,1)S(1)}, u32[]{:S(2)}, u32[]{:S(2)}) collective-permute-start(bf16[128,2176]{1,0:T(8,128)(2,1)S(1)} %pack.1.refs_0_.refs_3_), channel_id=1, source_target_pairs={{0,16},{2,18},{4,20},{6,22},{8,24},{10,26},{12,28},{14,30},{16,0},... | collective-permute-start | bytes 1671176 | tf_op jit(solution)/shard_map/ppermute | solution.py:424
  19.2 2.6 %forward0.1.after.refs_0_.refs_3_ = bf16[320,2048]{1,0:T(8,128)(2,1)S(1)} custom-call(s32[7]{0:T(128)S(1)} %stack.21.meta, bf16[4,4,80,768]{3,2,1,0:T(8,128)(2,1)S(1)} %bitcast.19, bf16[768,2048]{1,0:T(8,128)(2,1)S(1)} %bitcast.13, bf16[320,2048]{1,0:T(8,128)(2,1)S(1)} %forward3.1.refs_2_, bf16[128,2176]{1,0:T(8,128)(2,1)S(1)} %pack.1.refs_0_.refs_3_), custom_call_target="tpu_custom_call" | custom-call | flops 1024 | bytes 1024 | tf_op jit(solution)/shard_map/forward0/pallas_call | solution.py:19
  21.9 1.8 %turn.1 = (bf16[4,768,320]{2,1,0:T(8,128)(2,1)S(1)}, bf16[320,768]{1,0:T(8,128)(2,1)S(1)}, bf16[768,320]{1,0:T(8,128)(2,1)S(1)}) custom-call(s32[7]{0:T(128)S(1)} %stack.21.meta, bf16[4,4,80,768]{3,2,1,0:T(8,128)(2,1)S(1)} %bitcast.20, bf16[320,2048]{1,0:T(8,128)(2,1)S(1)} %forward0.1.after.refs_0_.refs_3_), custom_call_target="tpu_custom_call" | custom-call | flops 1024 | bytes 1024 | tf_op jit(solution)/shard_map/turn/pallas_call | solution.py:19
  23.7 1.9 %collective-permute-start.3 = (bf16[320,768]{1,0:T(8,128)(2,1)S(1)}, bf16[320,768]{1,0:T(8,128)(2,1)S(1)}, u32[]{:S(2)}, u32[]{:S(2)}) collective-permute-start(bf16[320,768]{1,0:T(8,128)(2,1)S(1)} %get-tuple-element.33), channel_id=1, source_target_pairs={{0,1},{1,0},{2,3},{3,2},{4,5},{5,4},{6,7},{7,6},{8,9},{9,8},{10,11... | collective-permute-start | bytes 1474568 | tf_op jit(solution)/shard_map/ppermute | solution.py:427
  25.6 1.5 %collective-permute-done.3.hidden = bf16[320,768]{1,0:T(8,128)(2,1)S(1)} collective-permute-done((bf16[320,768]{1,0:T(8,128)(2,1)S(1)}, bf16[320,768]{1,0:T(8,128)(2,1)S(1)}, u32[]{:S(2)}, u32[]{:S(2)}) %collective-permute-start.3) | collective-permute-done | bytes 491552 | tf_op jit(solution)/shard_map/ppermute | solution.py:427
  28.4 14.8 %collective-permute-done.1.refs_2_.refs_1_ = bf16[128,2176]{1,0:T(8,128)(2,1)S(1)} collective-permute-done((bf16[128,2176]{1,0:T(8,128)(2,1)S(1)}, bf16[128,2176]{1,0:T(8,128)(2,1)S(1)}, u32[]{:S(2)}, u32[]{:S(2)}) %collective-permute-start.1) | collective-permute-done | bytes 557088 | tf_op jit(solution)/shard_map/ppermute | solution.py:424
  43.2 1.6 %collective-permute-start.2 = (bf16[128,2176]{1,0:T(8,128)(2,1)S(1)}, bf16[128,2176]{1,0:T(8,128)(2,1)S(1)}, u32[]{:S(2)}, u32[]{:S(2)}) collective-permute-start(bf16[128,2176]{1,0:T(8,128)(2,1)S(1)} %collective-permute-done.1.refs_2_.refs_1_), channel_id=1, source_target_pairs={{0,8},{2,10},{4,12},{6,14},{8,0},{10,2},{12,4},{14,6},{16,24},{18,... | collective-permute-start | bytes 1671176 | tf_op jit(solution)/shard_map/ppermute | solution.py:424
  45.5 6.3 %collective-permute-done.refs_1_.refs_0_ = bf16[128,2176]{1,0:T(8,128)(2,1)S(1)} collective-permute-done((bf16[128,2176]{1,0:T(8,128)(2,1)S(1)}, bf16[128,2176]{1,0:T(8,128)(2,1)S(1)}, u32[]{:S(2)}, u32[]{:S(2)}) %collective-permute-start) | collective-permute-done | bytes 557088 | tf_op jit(solution)/shard_map/ppermute | solution.py:424
  51.8 11.9 %collective-permute-done.2.refs_3_.refs_1_ = bf16[128,2176]{1,0:T(8,128)(2,1)S(1)} collective-permute-done((bf16[128,2176]{1,0:T(8,128)(2,1)S(1)}, bf16[128,2176]{1,0:T(8,128)(2,1)S(1)}, u32[]{:S(2)}, u32[]{:S(2)}) %collective-permute-start.2) | collective-permute-done | bytes 557088 | tf_op jit(solution)/shard_map/ppermute | solution.py:424
  64.5 1.7 %own_rows.1 = (bf16[640,1024]{1,0:T(8,128)(2,1)S(1)}, bf16[320,1024]{1,0:T(8,128)(2,1)S(1)}, bf16[320,1024]{1,0:T(8,128)(2,1)S(1)}) custom-call(s32[7]{0:T(128)S(1)} %stack.21.meta, bf16[128,2176]{1,0:T(8,128)(2,1)S(1)} %pack.1.refs_0_.refs_3_, bf16[128,2176]{1,0:T(8,128)(2,1)S(1)} %collective-permute-done.refs_1_.refs_0_, ...), custom_call_target="tpu_custom_call" | custom-call | flops 1024 | bytes 1024 | tf_op jit(solution)/shard_map/own_rows/pallas_call | solution.py:36
  68.6 1.4 %collective-permute-start.8 = (bf16[528,1024]{1,0:T(8,128)(2,1)S(1)}, bf16[528,1024]{1,0:T(8,128)(2,1)S(1)}, u32[]{:S(2)}, u32[]{:S(2)}) collective-permute-start(bf16[528,1024]{1,0:T(8,128)(2,1)S(1)} %follow.3), channel_id=1, source_target_pairs={{0,4},{2,6},{4,0},{6,2},{8,12},{10,14},{12,8},{14,10},{16,20},{18,... | collective-permute-start | bytes 3244040 | tf_op jit(solution)/shard_map/ppermute | solution.py:424
  69.9 4.1 %combine1.1.refs_2_ = bf16[256,2176]{1,0:T(8,128)(2,1)S(1)} custom-call(s32[7]{0:T(128)S(1)} %stack.21.meta, bf16[128,2176]{1,0:T(8,128)(2,1)S(1)} %collective-permute-done.refs_1_.refs_0_, bf16[128,2176]{1,0:T(8,128)(2,1)S(1)} %collective-permute-done.2.refs_3_.refs_1_, bf16[640,1024]{1,0:T(8,128)(2,1)S(1)} %get-tuple-element.37.refs_2_.refs_0_, ...), custom_call_target="tpu_custom_call" | custom-call | flops 1024 | bytes 1024 | tf_op jit(solution)/shard_map/combine1/pallas_call | solution.py:36
  74.4 2.6 %inside0.1 = (bf16[4,4,80,768]{3,2,1,0:T(8,128)(2,1)}, f32[16,128]{1,0:T(8,128)S(1)}) custom-call(s32[7]{0:T(128)S(1)} %stack.21.meta, bf16[768,2048]{1,0:T(8,128)(2,1)S(1)} %bitcast.14, bf16[640,1024]{1,0:T(8,128)(2,1)S(1)} %get-tuple-element.37.refs_2_.refs_0_), custom_call_target="tpu_custom_call" | custom-call | flops 1024 | bytes 1024 | tf_op jit(solution)/shard_map/inside0/pallas_call | solution.py:36
  77.3 2.3 %weight_grad0.1 = (f32[768,1024]{1,0:T(8,128)S(1)}, f32[768,1024]{1,0:T(8,128)S(1)}, f32[16,128]{1,0:T(8,128)S(1)}) custom-call(s32[7]{0:T(128)S(1)} %stack.21.meta, bf16[4,768,320]{2,1,0:T(8,128)(2,1)S(1)} %get-tuple-element.38.turned, bf16[640,1024]{1,0:T(8,128)(2,1)S(1)} %get-tuple-element.37.refs_2_.refs_0_, f32[16,128]{1,0:T(8,128)S(1)} %get-tuple-element.39.refs_1_), custom_call_target="tpu_custom_call" | custom-call | flops 1024 | bytes 1024 | tf_op jit(solution)/shard_map/weight_grad0/pallas_call | solution.py:36
  79.6 4.1 %combine0.1.refs_2_ = f32[256,2176]{1,0:T(8,128)S(1)} custom-call(s32[7]{0:T(128)S(1)} %stack.21.meta, bf16[128,2176]{1,0:T(8,128)(2,1)S(1)} %pack.1.refs_0_.refs_3_, bf16[128,2176]{1,0:T(8,128)(2,1)S(1)} %collective-permute-done.1.refs_2_.refs_1_, bf16[256,2176]{1,0:T(8,128)(2,1)S(1)} %combine1.1.refs_2_, ...), custom_call_target="tpu_custom_call" | custom-call | flops 1024 | bytes 1024 | tf_op jit(solution)/shard_map/combine0/pallas_call | solution.py:36
  83.7 7.8 %collective-permute-done.7.refs_0_ = bf16[528,1024]{1,0:T(8,128)(2,1)S(1)} collective-permute-done((bf16[528,1024]{1,0:T(8,128)(2,1)S(1)}, bf16[528,1024]{1,0:T(8,128)(2,1)S(1)}, u32[]{:S(2)}, u32[]{:S(2)}) %collective-permute-start.7) | collective-permute-done | bytes 1081376 | tf_op jit(solution)/shard_map/ppermute | solution.py:424
  92.4 1.4 %near_rows.1 = (bf16[320,1024]{1,0:T(8,128)(2,1)S(1)}, bf16[320,1024]{1,0:T(8,128)(2,1)S(1)}, bf16[320,1024]{1,0:T(8,128)(2,1)S(1)}, bf16[320,1024]{1,0:T(8,128)(2,1)S(1)}) custom-call(s32[7]{0:T(128)S(1)} %stack.21.meta, bf16[528,1024]{1,0:T(8,128)(2,1)S(1)} %collective-permute-done.7.refs_0_, bf16[528,1024]{1,0:T(8,128)(2,1)S(1)} %collective-permute-done.8.refs_1_, ...), custom_call_target="tpu_custom_call" | custom-call | flops 10000000000 | bytes 1024 | tf_op jit(solution)/shard_map/near_rows/pallas_call | solution.py:36
  94.2 1.5 %collective-permute-start.9 = (bf16[320,1024]{1,0:T(8,128)(2,1)S(1)}, bf16[320,1024]{1,0:T(8,128)(2,1)S(1)}, u32[]{:S(2)}, u32[]{:S(2)}) collective-permute-start(bf16[320,1024]{1,0:T(8,128)(2,1)S(1)} %get-tuple-element.41), channel_id=1, source_target_pairs={{0,4},{2,6},{4,0},{6,2},{8,12},{10,14},{12,8},{14,10},{16,20},{18,... | collective-permute-start | bytes 1966088 | tf_op jit(solution)/shard_map/ppermute | solution.py:424
  95.7 2.8 %collective-permute-done.11 = bf16[256,2176]{1,0:T(8,128)(2,1)S(1)} collective-permute-done((bf16[256,2176]{1,0:T(8,128)(2,1)S(1)}, bf16[256,2176]{1,0:T(8,128)(2,1)S(1)}, u32[]{:S(2)}, u32[]{:S(2)}) %collective-permute-start.11) | collective-permute-done | bytes 1114144 | tf_op jit(solution)/shard_map/ppermute | solution.py:424
  99.1 7.4 %collective-permute-done.14.refs_2_ = bf16[320,1024]{1,0:T(8,128)(2,1)S(1)} collective-permute-done((bf16[320,1024]{1,0:T(8,128)(2,1)S(1)}, bf16[320,1024]{1,0:T(8,128)(2,1)S(1)}, u32[]{:S(2)}, u32[]{:S(2)}) %collective-permute-start.14) | collective-permute-done | bytes 655392 | tf_op jit(solution)/shard_map/ppermute | solution.py:424
  106.5 3.6 %inside1.1 = (bf16[4,4,80,768]{3,2,1,0:T(8,128)(2,1)}, f32[16,128]{1,0:T(8,128)S(1)}) custom-call(s32[7]{0:T(128)S(1)} %stack.21.meta, bf16[768,2048]{1,0:T(8,128)(2,1)S(1)} %bitcast.15, bf16[320,1024]{1,0:T(8,128)(2,1)S(1)} %get-tuple-element.44.refs_0_, bf16[320,1024]{1,0:T(8,128)(2,1)S(1)} %collective-permute-done.13.refs_1_, ...), custom_call_target="tpu_custom_call", output_to_operand_aliasing={{0}: (8, {})} | custom-call | flops 1024 | bytes 1024 | tf_op jit(solution)/shard_map/inside1/pallas_call | solution.py:36
  110.1 4.7 %weight_grad1.1 = (bf16[768,1024]{1,0:T(8,128)(2,1)S(1)}, f32[768,1024]{1,0:T(8,128)S(1)}, f32[16,128]{1,0:T(8,128)}) custom-call(s32[7]{0:T(128)S(1)} %stack.21.meta, bf16[4,768,320]{2,1,0:T(8,128)(2,1)S(1)} %get-tuple-element.38.turned, bf16[320,1024]{1,0:T(8,128)(2,1)S(1)} %get-tuple-element.44.refs_0_, ...), custom_call_target="tpu_custom_call" | custom-call | flops 1024 | bytes 1024 | tf_op jit(solution)/shard_map/weight_grad1/pallas_call | solution.py:36
  114.8 4.4 %collective-permute-start.16 = (bf16[768,1024]{1,0:T(8,128)(2,1)S(1)}, bf16[768,1024]{1,0:T(8,128)(2,1)S(1)}, u32[]{:S(2)}, u32[]{:S(2)}) collective-permute-start(bf16[768,1024]{1,0:T(8,128)(2,1)S(1)} %get-tuple-element.57), channel_id=1, source_target_pairs={{0,1},{1,0},{2,3},{3,2},{4,5},{5,4},{6,7},{7,6},{8,9},{9,8},{10,11... | collective-permute-start | bytes 4718600 | tf_op jit(solution)/shard_map/ppermute | solution.py:427
  120.5 2.4 %collective-permute-start.15 = (bf16[320,1024]{1,0:T(8,128)(2,1)S(1)}, bf16[320,1024]{1,0:T(8,128)(2,1)S(1)}, u32[]{:S(2)}, u32[]{:S(2)}) collective-permute-start(bf16[320,1024]{1,0:T(8,128)(2,1)S(1)} %collective-permute-done.9.refs_0_), channel_id=1, source_target_pairs={{0,1},{1,0},{2,3},{3,2},{4,5},{5,4},{6,7},{7,6},{8,9},{9,8},{10,11... | collective-permute-start | bytes 1966088 | tf_op jit(solution)/shard_map/ppermute | solution.py:427
  122.9 2.5 %collective-permute-done.12.refs_4_ = bf16[128,2176]{1,0:T(8,128)(2,1)S(1)} collective-permute-done((bf16[128,2176]{1,0:T(8,128)(2,1)S(1)}, bf16[128,2176]{1,0:T(8,128)(2,1)S(1)}, u32[]{:S(2)}, u32[]{:S(2)}) %collective-permute-start.12) | collective-permute-done | bytes 557088 | tf_op jit(solution)/shard_map/ppermute | solution.py:424
  125.4 4.1 %tail.1 = (bf16[4,4,80,768]{3,2,1,0:T(8,128)(2,1)}, bf16[128,2048]{1,0:T(8,128)(2,1)}, f32[8,128]{1,0:T(8,128)}, f32[768,1024]{1,0:T(8,128)S(1)}) custom-call(s32[7]{0:T(128)S(1)} %stack.21.meta, bf16[768,2048]{1,0:T(8,128)(2,1)S(1)} %bitcast.16, bf16[320,1024]{1,0:T(8,128)(2,1)S(1)} %collective-permute-done.9.refs_0_, ...), custom_call_target="tpu_custom_call", output_to_operand_aliasing={{0}: (9, {})} | custom-call | flops 99999997952 | bytes 1024 | tf_op jit(solution)/shard_map/tail/pallas_call | solution.py:36
  129.6 2.5 %last.1 = bf16[768,1024]{1,0:T(8,128)(2,1)} custom-call(s32[7]{0:T(128)S(1)} %stack.21.meta, bf16[768,320]{1,0:T(8,128)(2,1)S(1)} %turn_other.1.refs_1_.turned, bf16[320,1024]{1,0:T(8,128)(2,1)S(1)} %collective-permute-done.15.rows, f32[768,1024]{1,0:T(8,128)S(1)} %get-tuple-element.56.earlier, bf16[768,1024]{1,0:T(8,128)(2,1)S(1)} %collective-permute-done.16.earlier_other), custom_call_target="tpu_custom_call" | custom-call | flops 1024 | bytes 1024 | tf_op jit(solution)/shard_map/last/pallas_call | solution.py:36
  (38 shorter events, 12.3 us)
Async XLA Ops:
  0.6 8.6 %copy-start.4 = (f32[128,8]{0,1:T(8,128)S(1)}, f32[128,8]{0,1:T(8,128)}, u32[]{:S(2)}) copy-start(f32[128,8]{0,1:T(8,128)} %param.6) | copy-start | bytes 12292
  0.6 8.6 %copy-start.5 = (s32[128,8]{0,1:T(8,128)S(1)}, s32[128,8]{0,1:T(8,128)}, u32[]{:S(2)}) copy-start(s32[128,8]{0,1:T(8,128)} %param.5) | copy-start | bytes 12292
  0.7 10.5 %copy-start = (bf16[1,768,2048]{2,1,0:T(8,128)(2,1)S(1)}, bf16[1,768,2048]{2,1,0:T(8,128)(2,1)}, u32[]{:S(2)}) copy-start(bf16[1,768,2048]{2,1,0:T(8,128)(2,1)} %param.8) | copy-start | bytes 9437188
  5.8 60.3 %collective-permute-start.4 = (bf16[320,2048]{1,0:T(8,128)(2,1)}, bf16[320,2048]{1,0:T(8,128)(2,1)}, u32[]{:S(2)}, u32[]{:S(2)}) collective-permute-start(bf16[320,2048]{1,0:T(8,128)(2,1)} %get-tuple-element.35), channel_id=1, source_target_pairs={{0,2},{2,0},{4,6},{6,4},{8,10},{10,8},{12,14},{14,12},{16,18},{18,... | collective-permute-start | bytes 3932168 | tf_op jit(solution)/shard_map/ppermute | solution.py:424
  7.9 58.3 %collective-permute-start.5 = (bf16[320,2048]{1,0:T(8,128)(2,1)}, bf16[320,2048]{1,0:T(8,128)(2,1)}, u32[]{:S(2)}, u32[]{:S(2)}) collective-permute-start(bf16[320,2048]{1,0:T(8,128)(2,1)} %get-tuple-element.32.refs_2_), channel_id=1, source_target_pairs={{0,4},{2,6},{4,0},{6,2},{8,12},{10,14},{12,8},{14,10},{16,20},{18,... | collective-permute-start | bytes 3932168 | tf_op jit(solution)/shard_map/ppermute | solution.py:424
  9.3 1.0 copy-start.3
  11.2 1.5 %copy-start.1 = (bf16[1,1280,768]{2,1,0:T(8,128)(2,1)S(1)}, bf16[1,1280,768]{2,1,0:T(8,128)(2,1)}, u32[]{:S(2)}) copy-start(bf16[1,1280,768]{2,1,0:T(8,128)(2,1)} %param.7) | copy-start | bytes 5898244
  12.7 1.3 copy-start.2
  16.7 50.8 %collective-permute-start.6 = (bf16[320,2048]{1,0:T(8,128)(2,1)S(1)}, bf16[320,2048]{1,0:T(8,128)(2,1)S(1)}, u32[]{:S(2)}, u32[]{:S(2)}) collective-permute-start(bf16[320,2048]{1,0:T(8,128)(2,1)S(1)} %forward3.1.refs_2_), channel_id=1, source_target_pairs={{0,6},{2,4},{4,2},{6,0},{8,14},{10,12},{12,10},{14,8},{16,22},{18,... | collective-permute-start | bytes 3932168 | tf_op jit(solution)/shard_map/ppermute | solution.py:424
  16.8 26.4 %collective-permute-start.1 = (bf16[128,2176]{1,0:T(8,128)(2,1)S(1)}, bf16[128,2176]{1,0:T(8,128)(2,1)S(1)}, u32[]{:S(2)}, u32[]{:S(2)}) collective-permute-start(bf16[128,2176]{1,0:T(8,128)(2,1)S(1)} %pack.1.refs_0_.refs_3_), channel_id=1, source_target_pairs={{0,16},{2,18},{4,20},{6,22},{8,24},{10,26},{12,28},{14,30},{16,0},... | collective-permute-start | bytes 1671176 | tf_op jit(solution)/shard_map/ppermute | solution.py:424
  23.7 3.3 %collective-permute-start.3 = (bf16[320,768]{1,0:T(8,128)(2,1)S(1)}, bf16[320,768]{1,0:T(8,128)(2,1)S(1)}, u32[]{:S(2)}, u32[]{:S(2)}) collective-permute-start(bf16[320,768]{1,0:T(8,128)(2,1)S(1)} %get-tuple-element.33), channel_id=1, source_target_pairs={{0,1},{1,0},{2,3},{3,2},{4,5},{5,4},{6,7},{7,6},{8,9},{9,8},{10,11... | collective-permute-start | bytes 1474568 | tf_op jit(solution)/shard_map/ppermute | solution.py:427
  27.1 24.7 %collective-permute-start = (bf16[128,2176]{1,0:T(8,128)(2,1)S(1)}, bf16[128,2176]{1,0:T(8,128)(2,1)S(1)}, u32[]{:S(2)}, u32[]{:S(2)}) collective-permute-start(bf16[128,2176]{1,0:T(8,128)(2,1)S(1)} %pack.1.refs_0_.refs_3_), channel_id=1, source_target_pairs={{0,8},{2,10},{4,12},{6,14},{8,0},{10,2},{12,4},{14,6},{16,24},{18,... | collective-permute-start | bytes 1671176 | tf_op jit(solution)/shard_map/ppermute | solution.py:424
  43.2 20.6 %collective-permute-start.2 = (bf16[128,2176]{1,0:T(8,128)(2,1)S(1)}, bf16[128,2176]{1,0:T(8,128)(2,1)S(1)}, u32[]{:S(2)}, u32[]{:S(2)}) collective-permute-start(bf16[128,2176]{1,0:T(8,128)(2,1)S(1)} %collective-permute-done.1.refs_2_.refs_1_), channel_id=1, source_target_pairs={{0,8},{2,10},{4,12},{6,14},{8,0},{10,2},{12,4},{14,6},{16,24},{18,... | collective-permute-start | bytes 1671176 | tf_op jit(solution)/shard_map/ppermute | solution.py:424
  67.4 24.0 %collective-permute-start.7 = (bf16[528,1024]{1,0:T(8,128)(2,1)S(1)}, bf16[528,1024]{1,0:T(8,128)(2,1)S(1)}, u32[]{:S(2)}, u32[]{:S(2)}) collective-permute-start(bf16[528,1024]{1,0:T(8,128)(2,1)S(1)} %follow.2), channel_id=1, source_target_pairs={{0,2},{2,0},{4,6},{6,4},{8,10},{10,8},{12,14},{14,12},{16,18},{18,... | collective-permute-start | bytes 3244040 | tf_op jit(solution)/shard_map/ppermute | solution.py:424
  68.6 23.9 %collective-permute-start.8 = (bf16[528,1024]{1,0:T(8,128)(2,1)S(1)}, bf16[528,1024]{1,0:T(8,128)(2,1)S(1)}, u32[]{:S(2)}, u32[]{:S(2)}) collective-permute-start(bf16[528,1024]{1,0:T(8,128)(2,1)S(1)} %follow.3), channel_id=1, source_target_pairs={{0,4},{2,6},{4,0},{6,2},{8,12},{10,14},{12,8},{14,10},{16,20},{18,... | collective-permute-start | bytes 3244040 | tf_op jit(solution)/shard_map/ppermute | solution.py:424
  74.0 24.5 %collective-permute-start.11 = (bf16[256,2176]{1,0:T(8,128)(2,1)S(1)}, bf16[256,2176]{1,0:T(8,128)(2,1)S(1)}, u32[]{:S(2)}, u32[]{:S(2)}) collective-permute-start(bf16[256,2176]{1,0:T(8,128)(2,1)S(1)} %combine1.1.refs_2_), channel_id=1, source_target_pairs={{0,8},{2,10},{4,12},{6,14},{8,0},{10,2},{12,4},{14,6},{16,24},{18,... | collective-permute-start | bytes 3342344 | tf_op jit(solution)/shard_map/ppermute | solution.py:424
  74.1 32.4 %collective-permute-start.13 = (bf16[320,1024]{1,0:T(8,128)(2,1)S(1)}, bf16[320,1024]{1,0:T(8,128)(2,1)S(1)}, u32[]{:S(2)}, u32[]{:S(2)}) collective-permute-start(bf16[320,1024]{1,0:T(8,128)(2,1)S(1)} %get-tuple-element.34.refs_2_), channel_id=1, source_target_pairs={{0,2},{2,0},{4,6},{6,4},{8,10},{10,8},{12,14},{14,12},{16,18},{18,... | collective-permute-start | bytes 1966088 | tf_op jit(solution)/shard_map/ppermute | solution.py:424
  77.0 29.5 %collective-permute-start.14 = (bf16[320,1024]{1,0:T(8,128)(2,1)S(1)}, bf16[320,1024]{1,0:T(8,128)(2,1)S(1)}, u32[]{:S(2)}, u32[]{:S(2)}) collective-permute-start(bf16[320,1024]{1,0:T(8,128)(2,1)S(1)} %get-tuple-element.45), channel_id=1, source_target_pairs={{0,4},{2,6},{4,0},{6,2},{8,12},{10,14},{12,8},{14,10},{16,20},{18,... | collective-permute-start | bytes 1966088 | tf_op jit(solution)/shard_map/ppermute | solution.py:424
  93.9 31.6 %collective-permute-start.10 = (bf16[320,1024]{1,0:T(8,128)(2,1)S(1)}, bf16[320,1024]{1,0:T(8,128)(2,1)S(1)}, u32[]{:S(2)}, u32[]{:S(2)}) collective-permute-start(bf16[320,1024]{1,0:T(8,128)(2,1)S(1)} %get-tuple-element.42), channel_id=1, source_target_pairs={{0,2},{2,0},{4,6},{6,4},{8,10},{10,8},{12,14},{14,12},{16,18},{18,... | collective-permute-start | bytes 1966088 | tf_op jit(solution)/shard_map/ppermute | solution.py:424
  94.2 26.3 %collective-permute-start.9 = (bf16[320,1024]{1,0:T(8,128)(2,1)S(1)}, bf16[320,1024]{1,0:T(8,128)(2,1)S(1)}, u32[]{:S(2)}, u32[]{:S(2)}) collective-permute-start(bf16[320,1024]{1,0:T(8,128)(2,1)S(1)} %get-tuple-element.41), channel_id=1, source_target_pairs={{0,4},{2,6},{4,0},{6,2},{8,12},{10,14},{12,8},{14,10},{16,20},{18,... | collective-permute-start | bytes 1966088 | tf_op jit(solution)/shard_map/ppermute | solution.py:424
  98.7 26.7 %collective-permute-start.12 = (bf16[128,2176]{1,0:T(8,128)(2,1)S(1)}, bf16[128,2176]{1,0:T(8,128)(2,1)S(1)}, u32[]{:S(2)}, u32[]{:S(2)}) collective-permute-start(bf16[128,2176]{1,0:T(8,128)(2,1)S(1)} %get-tuple-element.58), channel_id=1, source_target_pairs={{0,16},{2,18},{4,20},{6,22},{8,24},{10,26},{12,28},{14,30},{16,0},... | collective-permute-start | bytes 1671176 | tf_op jit(solution)/shard_map/ppermute | solution.py:424
  114.8 14.8 %collective-permute-start.16 = (bf16[768,1024]{1,0:T(8,128)(2,1)S(1)}, bf16[768,1024]{1,0:T(8,128)(2,1)S(1)}, u32[]{:S(2)}, u32[]{:S(2)}) collective-permute-start(bf16[768,1024]{1,0:T(8,128)(2,1)S(1)} %get-tuple-element.57), channel_id=1, source_target_pairs={{0,1},{1,0},{2,3},{3,2},{4,5},{5,4},{6,7},{7,6},{8,9},{9,8},{10,11... | collective-permute-start | bytes 4718600 | tf_op jit(solution)/shard_map/ppermute | solution.py:427
  120.5 9.0 %collective-permute-start.15 = (bf16[320,1024]{1,0:T(8,128)(2,1)S(1)}, bf16[320,1024]{1,0:T(8,128)(2,1)S(1)}, u32[]{:S(2)}, u32[]{:S(2)}) collective-permute-start(bf16[320,1024]{1,0:T(8,128)(2,1)S(1)} %collective-permute-done.9.refs_0_), channel_id=1, source_target_pairs={{0,1},{1,0},{2,3},{3,2},{4,5},{5,4},{6,7},{7,6},{8,9},{9,8},{10,11... | collective-permute-start | bytes 1966088 | tf_op jit(solution)/shard_map/ppermute | solution.py:427

commit v2 on v1

--- a/solution.py
+++ b/solution.py
@@ -149,7 +149,8 @@
         copy.wait()
 
 
-def turn_body(meta, hidden, after, out, final, final_turned):
+def turn_body(meta, hidden, *refs):
+    out, final, final_turned = refs[-3:]
     value = hidden[:, 0].reshape(final.shape)
     out[0] = value.T
     final[...] = value
@@ -437,21 +438,6 @@
     extent = -(-4 * count // 128) * 128
     short = pl.BlockSpec((top, tokens), lambda i, m: (0, 0))
     relay = peers == 4 and fold == 1 and planes * tokens <= large
-    packed = call(
-        pack_body, "pack", (1,),
-        [short, short, pl.BlockSpec((tokens, width), lambda i, m: (0, 0))],
-        pl.BlockSpec((tokens, width + extent), lambda i, m: (0, 0)),
-        jax.ShapeDtypeStruct((tokens, width + extent), BF16),
-        meta, (ids_turned, gates.T, out_grad),
-        room=room,
-    )
-    gathered = [packed]
-    for k in range(1, planes):
-        if k & (k - 1) == 0:
-            gathered.append(swap(packed, peers * k))
-        else:
-            gathered.append(None)
-
     def forward(peer, after):
         return call(
             lambda meta, *refs: forward_body(meta, refs[0], refs[1], refs[-1]), f"forward{peer}", (steps,),
@@ -480,21 +466,37 @@
             out_specs=[anywhere, anywhere],
             places={0: anywhere, 1: anywhere}, room=3.75,
         )
-        after = (outputs[2], packed)
+    packed = call(
+        lambda meta, *refs: pack_body(meta, *refs[:3], refs[-1]), "pack", (1,),
+        [short, short, pl.BlockSpec((tokens, width), lambda i, m: (0, 0))] + [glance] * relay,
+        pl.BlockSpec((tokens, width + extent), lambda i, m: (0, 0)),
+        jax.ShapeDtypeStruct((tokens, width + extent), BF16),
+        meta, (ids_turned, gates.T, out_grad, *([outputs[2]] if relay else [])),
+        room=room,
+    )
+    gathered = [packed]
+    for k in range(1, planes):
+        if k & (k - 1) == 0:
+            gathered.append(swap(packed, peers * k))
+        else:
+            gathered.append(None)
+
+    after = (outputs[2], packed) if relay else ()
     for peer in [peer for peer in list(range(1, peers)) + [0] if peer not in outputs]:
         outputs[peer] = forward(peer, after)
         after = (outputs[peer], packed)
     returned = [outputs[0]] + [swap(outputs[peer], peer) for peer in range(1, peers)]
+    waits = gathered[1:3] if relay else [outputs[0]]
     turned, hidden_last, turned_last = call(
         turn_body, "turn", (peers,),
-        [pl.BlockSpec(block, lambda i, m: (0, lax.bitwise_xor(m[0], i), 0, 0)), glance],
+        [pl.BlockSpec(block, lambda i, m: (0, lax.bitwise_xor(m[0], i), 0, 0))] + [glance] * len(waits),
         [pl.BlockSpec((1, inside, rows), lambda i, m: (i, 0, 0)), pl.BlockSpec((rows, inside), lambda i, m: (0, 0)),
          pl.BlockSpec((inside, rows), lambda i, m: (0, 0))],
         [
             jax.ShapeDtypeStruct((peers, inside, rows), BF16), jax.ShapeDtypeStruct((rows, inside), BF16),
             jax.ShapeDtypeStruct((inside, rows), BF16),
         ],
-        meta, (blocks, outputs[0]),
+        meta, (blocks, *waits),
     )
 
     turned_other = call(

time: 133 us -> 129 us (0.970)
  waiting for transfers between devices: 57.3 us -> 52.1 us
  starting transfers between devices: 22.8 us -> 25.1 us
  local copies, waits for them, and re-layouts: 3.99 us -> 2.6 us
    ppermute x14, waiting for transfers between devices: 55.8 us -> 52.1 us  [swap(): lax.ppermute(value, 'expert', [(e, e ^ distance) for e in range(count)])]
    ppermute x14, starting transfers between devices: 14.1 us -> 15.9 us  [swap(): lax.ppermute(value, 'expert', [(e, e ^ distance) for e in range(count)])]
    ppermute x3, waiting for transfers between devices: 1.5 us -> 0.01 us  [exchange(): return lax.ppermute(value, 'dp', [(0, 1), (1, 0)])]
    unnamed x12, local copies, waits for them, and re-layouts: 3.91 us -> 2.51 us
  transfers between devices with their start and end apart: 17 -> 17, of which waited for: 10 -> 8; matrix products, arithmetic and copies ran while one was open for 0% -> 0% of each run, Pallas kernels for 30% -> 31%
where the time goes in v2:
time: 129 us; the launch traced here: 128 us
  waiting for transfers between devices  52.1 us (40%)
  Pallas kernels  47 us (36%)
  starting transfers between devices  25.1 us (19%)
  local copies, waits for them, and re-layouts  2.6 us (2%)
    ppermute x14, waiting for transfers between devices, swap(): lax.ppermute(value, 'expert', [(e, e ^ distance) for e in range(count)])  52.1 us
    pallas_call x12, Pallas kernels, direct(): pl.pallas_call(body, name=name, in_specs=[smem] + [places.get(at, vmem) f...  37.1 us
    ppermute x14, starting transfers between devices, swap(): lax.ppermute(value, 'expert', [(e, e ^ distance) for e in range(count)])  15.9 us
    pallas_call x6, Pallas kernels, call(): pl.pallas_call(body, name=name, grid_spec=pltpu.PrefetchScalarGridSpec(nu...  9.92 us
    ppermute x3, starting transfers between devices, exchange(): return lax.ppermute(value, 'dp', [(0, 1), (1, 0)])  9.27 us
  transfers between devices with their start and end apart: 17, of which 8 were waited for; matrix products, arithmetic and copies ran while one was open for 0% of the time, Pallas kernels for 31%

profile of v2, /device:TPU:1, one launch (start us, length us, event | category | flops | bytes accessed | tf_op | source)
XLA Modules:
  0.0 128.1 jit_solution(17017626384257962932)
XLA Ops:
  0.7 5.2 %forward1.1 = (bf16[320,2048]{1,0:T(8,128)(2,1)}, bf16[320,2048]{1,0:T(8,128)(2,1)}) custom-call(s32[1]{0:T(128)} %bitcast.2.meta, bf16[4,4,80,768]{3,2,1,0:T(8,128)(2,1)} %bitcast.17, bf16[768,2048]{1,0:T(8,128)(2,1)} %bitcast.11), custom_call_target="tpu_custom_call" | custom-call | flops 1024 | bytes 1024 | tf_op jit(solution)/shard_map/forward1/pallas_call | solution.py:36
  5.8 2.1 %collective-permute-start.4 = (bf16[320,2048]{1,0:T(8,128)(2,1)}, bf16[320,2048]{1,0:T(8,128)(2,1)}, u32[]{:S(2)}, u32[]{:S(2)}) collective-permute-start(bf16[320,2048]{1,0:T(8,128)(2,1)} %get-tuple-element.35), channel_id=1, source_target_pairs={{0,2},{2,0},{4,6},{6,4},{8,10},{10,8},{12,14},{14,12},{16,18},{18,... | collective-permute-start | bytes 3932168 | tf_op jit(solution)/shard_map/ppermute | solution.py:425
  7.9 1.2 collective-permute-start.5
  9.3 1.4 %copy-done.2 = bf16[320,2048]{1,0:T(8,128)(2,1)S(1)} copy-done((bf16[320,2048]{1,0:T(8,128)(2,1)S(1)}, bf16[320,2048]{1,0:T(8,128)(2,1)}, u32[]{:S(2)}) %copy-start.2) | copy-done | bytes 1310744
  12.6 2.6 %forward3.1.refs_2_ = bf16[320,2048]{1,0:T(8,128)(2,1)S(1)} custom-call(s32[7]{0:T(128)S(1)} %stack.21.meta, bf16[4,4,80,768]{3,2,1,0:T(8,128)(2,1)S(1)} %bitcast.18, bf16[768,2048]{1,0:T(8,128)(2,1)S(1)} %bitcast.12, bf16[320,2048]{1,0:T(8,128)(2,1)S(1)} %copy-done.2, bf16[128,2176]{1,0:T(8,128)(2,1)S(1)} %pack.1.refs_0_.refs_3_), custom_call_target="tpu_custom_call" | custom-call | flops 1024 | bytes 1024 | tf_op jit(solution)/shard_map/forward3/pallas_call | solution.py:19
  15.4 2.5 %collective-permute-start.1 = (bf16[128,2176]{1,0:T(8,128)(2,1)S(1)}, bf16[128,2176]{1,0:T(8,128)(2,1)S(1)}, u32[]{:S(2)}, u32[]{:S(2)}) collective-permute-start(bf16[128,2176]{1,0:T(8,128)(2,1)S(1)} %pack.1.refs_0_.refs_3_), channel_id=1, source_target_pairs={{0,16},{2,18},{4,20},{6,22},{8,24},{10,26},{12,28},{14,30},{16,0},... | collective-permute-start | bytes 1671176 | tf_op jit(solution)/shard_map/ppermute | solution.py:425
  17.9 1.3 %collective-permute-start = (bf16[128,2176]{1,0:T(8,128)(2,1)S(1)}, bf16[128,2176]{1,0:T(8,128)(2,1)S(1)}, u32[]{:S(2)}, u32[]{:S(2)}) collective-permute-start(bf16[128,2176]{1,0:T(8,128)(2,1)S(1)} %pack.1.refs_0_.refs_3_), channel_id=1, source_target_pairs={{0,8},{2,10},{4,12},{6,14},{8,0},{10,2},{12,4},{14,6},{16,24},{18,... | collective-permute-start | bytes 1671176 | tf_op jit(solution)/shard_map/ppermute | solution.py:425
  19.2 22.6 %collective-permute-done.1.refs_2_.refs_1_ = bf16[128,2176]{1,0:T(8,128)(2,1)S(1)} collective-permute-done((bf16[128,2176]{1,0:T(8,128)(2,1)S(1)}, bf16[128,2176]{1,0:T(8,128)(2,1)S(1)}, u32[]{:S(2)}, u32[]{:S(2)}) %collective-permute-start.1) | collective-permute-done | bytes 557088 | tf_op jit(solution)/shard_map/ppermute | solution.py:425
  41.8 1.5 %collective-permute-start.2 = (bf16[128,2176]{1,0:T(8,128)(2,1)S(1)}, bf16[128,2176]{1,0:T(8,128)(2,1)S(1)}, u32[]{:S(2)}, u32[]{:S(2)}) collective-permute-start(bf16[128,2176]{1,0:T(8,128)(2,1)S(1)} %collective-permute-done.1.refs_2_.refs_1_), channel_id=1, source_target_pairs={{0,8},{2,10},{4,12},{6,14},{8,0},{10,2},{12,4},{14,6},{16,24},{18,... | collective-permute-start | bytes 1671176 | tf_op jit(solution)/shard_map/ppermute | solution.py:425
  43.3 1.7 %turn.1 = (bf16[4,768,320]{2,1,0:T(8,128)(2,1)S(1)}, bf16[320,768]{1,0:T(8,128)(2,1)S(1)}, bf16[768,320]{1,0:T(8,128)(2,1)S(1)}) custom-call(s32[7]{0:T(128)S(1)} %stack.21.meta, bf16[4,4,80,768]{3,2,1,0:T(8,128)(2,1)S(1)} %bitcast.19, bf16[128,2176]{1,0:T(8,128)(2,1)S(1)} %collective-permute-done.refs_1_.refs_0_, ...), custom_call_target="tpu_custom_call" | custom-call | flops 1024 | bytes 1024 | tf_op jit(solution)/shard_map/turn/pallas_call | solution.py:19
  45.8 2.8 %forward0.1.refs_0_.refs_3_ = bf16[320,2048]{1,0:T(8,128)(2,1)S(1)} custom-call(s32[7]{0:T(128)S(1)} %stack.21.meta, bf16[4,4,80,768]{3,2,1,0:T(8,128)(2,1)S(1)} %bitcast.20, bf16[768,2048]{1,0:T(8,128)(2,1)S(1)} %bitcast.13, bf16[320,2048]{1,0:T(8,128)(2,1)S(1)} %forward3.1.refs_2_, bf16[128,2176]{1,0:T(8,128)(2,1)S(1)} %pack.1.refs_0_.refs_3_), custom_call_target="tpu_custom_call" | custom-call | flops 1024 | bytes 1024 | tf_op jit(solution)/shard_map/forward0/pallas_call | solution.py:19
  49.4 5.4 %collective-permute-done.2.refs_3_.refs_1_ = bf16[128,2176]{1,0:T(8,128)(2,1)S(1)} collective-permute-done((bf16[128,2176]{1,0:T(8,128)(2,1)S(1)}, bf16[128,2176]{1,0:T(8,128)(2,1)S(1)}, u32[]{:S(2)}, u32[]{:S(2)}) %collective-permute-start.2) | collective-permute-done | bytes 557088 | tf_op jit(solution)/shard_map/ppermute | solution.py:425
  55.6 1.7 %own_rows.1 = (bf16[640,1024]{1,0:T(8,128)(2,1)S(1)}, bf16[320,1024]{1,0:T(8,128)(2,1)S(1)}, bf16[320,1024]{1,0:T(8,128)(2,1)S(1)}) custom-call(s32[7]{0:T(128)S(1)} %stack.21.meta, bf16[128,2176]{1,0:T(8,128)(2,1)S(1)} %pack.1.refs_0_.refs_3_, bf16[128,2176]{1,0:T(8,128)(2,1)S(1)} %collective-permute-done.refs_1_.refs_0_, ...), custom_call_target="tpu_custom_call" | custom-call | flops 1024 | bytes 1024 | tf_op jit(solution)/shard_map/own_rows/pallas_call | solution.py:36
  58.5 7.2 %collective-permute-done.6.refs_2_.refs_6_ = bf16[320,2048]{1,0:T(8,128)(2,1)S(1)} collective-permute-done((bf16[320,2048]{1,0:T(8,128)(2,1)S(1)}, bf16[320,2048]{1,0:T(8,128)(2,1)S(1)}, u32[]{:S(2)}, u32[]{:S(2)}) %collective-permute-start.6) | collective-permute-done | bytes 1310752 | tf_op jit(solution)/shard_map/ppermute | solution.py:425
  67.1 4.1 %combine1.1.refs_2_ = bf16[256,2176]{1,0:T(8,128)(2,1)S(1)} custom-call(s32[7]{0:T(128)S(1)} %stack.21.meta, bf16[128,2176]{1,0:T(8,128)(2,1)S(1)} %collective-permute-done.refs_1_.refs_0_, bf16[128,2176]{1,0:T(8,128)(2,1)S(1)} %collective-permute-done.2.refs_3_.refs_1_, bf16[640,1024]{1,0:T(8,128)(2,1)S(1)} %get-tuple-element.37.refs_2_.refs_0_, ...), custom_call_target="tpu_custom_call" | custom-call | flops 1024 | bytes 1024 | tf_op jit(solution)/shard_map/combine1/pallas_call | solution.py:36
  71.2 1.4 %collective-permute-start.11 = (bf16[256,2176]{1,0:T(8,128)(2,1)S(1)}, bf16[256,2176]{1,0:T(8,128)(2,1)S(1)}, u32[]{:S(2)}, u32[]{:S(2)}) collective-permute-start(bf16[256,2176]{1,0:T(8,128)(2,1)S(1)} %combine1.1.refs_2_), channel_id=1, source_target_pairs={{0,8},{2,10},{4,12},{6,14},{8,0},{10,2},{12,4},{14,6},{16,24},{18,... | collective-permute-start | bytes 3342344 | tf_op jit(solution)/shard_map/ppermute | solution.py:425
  72.8 2.6 %inside0.1 = (bf16[4,4,80,768]{3,2,1,0:T(8,128)(2,1)}, f32[16,128]{1,0:T(8,128)S(1)}) custom-call(s32[7]{0:T(128)S(1)} %stack.21.meta, bf16[768,2048]{1,0:T(8,128)(2,1)S(1)} %bitcast.14, bf16[640,1024]{1,0:T(8,128)(2,1)S(1)} %get-tuple-element.37.refs_2_.refs_0_), custom_call_target="tpu_custom_call" | custom-call | flops 1024 | bytes 1024 | tf_op jit(solution)/shard_map/inside0/pallas_call | solution.py:36
  75.4 1.3 %collective-permute-start.14 = (bf16[320,1024]{1,0:T(8,128)(2,1)S(1)}, bf16[320,1024]{1,0:T(8,128)(2,1)S(1)}, u32[]{:S(2)}, u32[]{:S(2)}) collective-permute-start(bf16[320,1024]{1,0:T(8,128)(2,1)S(1)} %get-tuple-element.45), channel_id=1, source_target_pairs={{0,4},{2,6},{4,0},{6,2},{8,12},{10,14},{12,8},{14,10},{16,20},{18,... | collective-permute-start | bytes 1966088 | tf_op jit(solution)/shard_map/ppermute | solution.py:425
  76.7 2.3 %weight_grad0.1 = (f32[768,1024]{1,0:T(8,128)S(1)}, f32[768,1024]{1,0:T(8,128)S(1)}, f32[16,128]{1,0:T(8,128)S(1)}) custom-call(s32[7]{0:T(128)S(1)} %stack.21.meta, bf16[4,768,320]{2,1,0:T(8,128)(2,1)S(1)} %get-tuple-element.38.turned, bf16[640,1024]{1,0:T(8,128)(2,1)S(1)} %get-tuple-element.37.refs_2_.refs_0_, f32[16,128]{1,0:T(8,128)S(1)} %get-tuple-element.39.refs_1_), custom_call_target="tpu_custom_call" | custom-call | flops 1024 | bytes 1024 | tf_op jit(solution)/shard_map/weight_grad0/pallas_call | solution.py:36
  79.0 4.1 %combine0.1.refs_2_ = f32[256,2176]{1,0:T(8,128)S(1)} custom-call(s32[7]{0:T(128)S(1)} %stack.21.meta, bf16[128,2176]{1,0:T(8,128)(2,1)S(1)} %pack.1.refs_0_.refs_3_, bf16[128,2176]{1,0:T(8,128)(2,1)S(1)} %collective-permute-done.1.refs_2_.refs_1_, bf16[256,2176]{1,0:T(8,128)(2,1)S(1)} %combine1.1.refs_2_, bf16[320,2048]{1,0:T(8,128)(2,1)S(1)} %forward0.1.refs_0_.refs_3_, ...), custom_call_target="tpu_custom_call" | custom-call | flops 1024 | bytes 1024 | tf_op jit(solution)/shard_map/combine0/pallas_call | solution.py:36
  83.1 5.2 %collective-permute-done.7.refs_0_ = bf16[528,1024]{1,0:T(8,128)(2,1)S(1)} collective-permute-done((bf16[528,1024]{1,0:T(8,128)(2,1)S(1)}, bf16[528,1024]{1,0:T(8,128)(2,1)S(1)}, u32[]{:S(2)}, u32[]{:S(2)}) %collective-permute-start.7) | collective-permute-done | bytes 1081376 | tf_op jit(solution)/shard_map/ppermute | solution.py:425
  88.3 1.8 %collective-permute-done.8.refs_1_ = bf16[528,1024]{1,0:T(8,128)(2,1)S(1)} collective-permute-done((bf16[528,1024]{1,0:T(8,128)(2,1)S(1)}, bf16[528,1024]{1,0:T(8,128)(2,1)S(1)}, u32[]{:S(2)}, u32[]{:S(2)}) %collective-permute-start.8) | collective-permute-done | bytes 1081376 | tf_op jit(solution)/shard_map/ppermute | solution.py:425
  90.2 1.4 %near_rows.1 = (bf16[320,1024]{1,0:T(8,128)(2,1)S(1)}, bf16[320,1024]{1,0:T(8,128)(2,1)S(1)}, bf16[320,1024]{1,0:T(8,128)(2,1)S(1)}, bf16[320,1024]{1,0:T(8,128)(2,1)S(1)}) custom-call(s32[7]{0:T(128)S(1)} %stack.21.meta, bf16[528,1024]{1,0:T(8,128)(2,1)S(1)} %collective-permute-done.7.refs_0_, bf16[528,1024]{1,0:T(8,128)(2,1)S(1)} %collective-permute-done.8.refs_1_, ...), custom_call_target="tpu_custom_call" | custom-call | flops 10000000000 | bytes 1024 | tf_op jit(solution)/shard_map/near_rows/pallas_call | solution.py:36
  92.0 1.6 %collective-permute-done.11 = bf16[256,2176]{1,0:T(8,128)(2,1)S(1)} collective-permute-done((bf16[256,2176]{1,0:T(8,128)(2,1)S(1)}, bf16[256,2176]{1,0:T(8,128)(2,1)S(1)}, u32[]{:S(2)}, u32[]{:S(2)}) %collective-permute-start.11) | collective-permute-done | bytes 1114144 | tf_op jit(solution)/shard_map/ppermute | solution.py:425
  93.9 2.3 %collective-permute-start.12 = (bf16[128,2176]{1,0:T(8,128)(2,1)S(1)}, bf16[128,2176]{1,0:T(8,128)(2,1)S(1)}, u32[]{:S(2)}, u32[]{:S(2)}) collective-permute-start(bf16[128,2176]{1,0:T(8,128)(2,1)S(1)} %get-tuple-element.58), channel_id=1, source_target_pairs={{0,16},{2,18},{4,20},{6,22},{8,24},{10,26},{12,28},{14,30},{16,0},... | collective-permute-start | bytes 1671176 | tf_op jit(solution)/shard_map/ppermute | solution.py:425
  96.2 8.0 %collective-permute-done.14.refs_2_ = bf16[320,1024]{1,0:T(8,128)(2,1)S(1)} collective-permute-done((bf16[320,1024]{1,0:T(8,128)(2,1)S(1)}, bf16[320,1024]{1,0:T(8,128)(2,1)S(1)}, u32[]{:S(2)}, u32[]{:S(2)}) %collective-permute-start.14) | collective-permute-done | bytes 655392 | tf_op jit(solution)/shard_map/ppermute | solution.py:425
  104.2 3.6 %inside1.1 = (bf16[4,4,80,768]{3,2,1,0:T(8,128)(2,1)}, f32[16,128]{1,0:T(8,128)S(1)}) custom-call(s32[7]{0:T(128)S(1)} %stack.21.meta, bf16[768,2048]{1,0:T(8,128)(2,1)S(1)} %bitcast.15, bf16[320,1024]{1,0:T(8,128)(2,1)S(1)} %get-tuple-element.44.refs_0_, bf16[320,1024]{1,0:T(8,128)(2,1)S(1)} %collective-permute-done.13.refs_1_, ...), custom_call_target="tpu_custom_call", output_to_operand_aliasing={{0}: (8, {})} | custom-call | flops 1024 | bytes 1024 | tf_op jit(solution)/shard_map/inside1/pallas_call | solution.py:36
  107.8 4.7 %weight_grad1.1 = (bf16[768,1024]{1,0:T(8,128)(2,1)S(1)}, f32[768,1024]{1,0:T(8,128)S(1)}, f32[16,128]{1,0:T(8,128)}) custom-call(s32[7]{0:T(128)S(1)} %stack.21.meta, bf16[4,768,320]{2,1,0:T(8,128)(2,1)S(1)} %get-tuple-element.38.turned, bf16[320,1024]{1,0:T(8,128)(2,1)S(1)} %get-tuple-element.44.refs_0_, ...), custom_call_target="tpu_custom_call" | custom-call | flops 1024 | bytes 1024 | tf_op jit(solution)/shard_map/weight_grad1/pallas_call | solution.py:36
  112.5 5.5 %collective-permute-start.16 = (bf16[768,1024]{1,0:T(8,128)(2,1)S(1)}, bf16[768,1024]{1,0:T(8,128)(2,1)S(1)}, u32[]{:S(2)}, u32[]{:S(2)}) collective-permute-start(bf16[768,1024]{1,0:T(8,128)(2,1)S(1)} %get-tuple-element.57), channel_id=1, source_target_pairs={{0,1},{1,0},{2,3},{3,2},{4,5},{5,4},{6,7},{7,6},{8,9},{9,8},{10,11... | collective-permute-start | bytes 4718600 | tf_op jit(solution)/shard_map/ppermute | solution.py:428
  118.3 2.9 %collective-permute-start.15 = (bf16[320,1024]{1,0:T(8,128)(2,1)S(1)}, bf16[320,1024]{1,0:T(8,128)(2,1)S(1)}, u32[]{:S(2)}, u32[]{:S(2)}) collective-permute-start(bf16[320,1024]{1,0:T(8,128)(2,1)S(1)} %collective-permute-done.9.refs_0_), channel_id=1, source_target_pairs={{0,1},{1,0},{2,3},{3,2},{4,5},{5,4},{6,7},{7,6},{8,9},{9,8},{10,11... | collective-permute-start | bytes 1966088 | tf_op jit(solution)/shard_map/ppermute | solution.py:428
  121.2 4.1 %tail.1 = (bf16[4,4,80,768]{3,2,1,0:T(8,128)(2,1)}, bf16[128,2048]{1,0:T(8,128)(2,1)}, f32[8,128]{1,0:T(8,128)}, f32[768,1024]{1,0:T(8,128)S(1)}) custom-call(s32[7]{0:T(128)S(1)} %stack.21.meta, bf16[768,2048]{1,0:T(8,128)(2,1)S(1)} %bitcast.16, bf16[320,1024]{1,0:T(8,128)(2,1)S(1)} %collective-permute-done.9.refs_0_, ...), custom_call_target="tpu_custom_call", output_to_operand_aliasing={{0}: (9, {})} | custom-call | flops 99999997952 | bytes 1024 | tf_op jit(solution)/shard_map/tail/pallas_call | solution.py:36
  125.3 2.6 %last.1 = bf16[768,1024]{1,0:T(8,128)(2,1)} custom-call(s32[7]{0:T(128)S(1)} %stack.21.meta, bf16[768,320]{1,0:T(8,128)(2,1)S(1)} %turn_other.1.refs_1_.turned, bf16[320,1024]{1,0:T(8,128)(2,1)S(1)} %collective-permute-done.15.rows, f32[768,1024]{1,0:T(8,128)S(1)} %get-tuple-element.56.earlier, bf16[768,1024]{1,0:T(8,128)(2,1)S(1)} %collective-permute-done.16.earlier_other), custom_call_target="tpu_custom_call" | custom-call | flops 1024 | bytes 1024 | tf_op jit(solution)/shard_map/last/pallas_call | solution.py:36
  (38 shorter events, 8.2 us)
Async XLA Ops:
  0.6 8.6 %copy-start.4 = (f32[128,8]{0,1:T(8,128)S(1)}, f32[128,8]{0,1:T(8,128)}, u32[]{:S(2)}) copy-start(f32[128,8]{0,1:T(8,128)} %param.6) | copy-start | bytes 12292
  0.6 8.6 %copy-start.5 = (s32[128,8]{0,1:T(8,128)S(1)}, s32[128,8]{0,1:T(8,128)}, u32[]{:S(2)}) copy-start(s32[128,8]{0,1:T(8,128)} %param.5) | copy-start | bytes 12292
  0.7 12.0 %copy-start = (bf16[1,768,2048]{2,1,0:T(8,128)(2,1)S(1)}, bf16[1,768,2048]{2,1,0:T(8,128)(2,1)}, u32[]{:S(2)}) copy-start(bf16[1,768,2048]{2,1,0:T(8,128)(2,1)} %param.8) | copy-start | bytes 9437188
  5.8 51.4 %collective-permute-start.4 = (bf16[320,2048]{1,0:T(8,128)(2,1)}, bf16[320,2048]{1,0:T(8,128)(2,1)}, u32[]{:S(2)}, u32[]{:S(2)}) collective-permute-start(bf16[320,2048]{1,0:T(8,128)(2,1)} %get-tuple-element.35), channel_id=1, source_target_pairs={{0,2},{2,0},{4,6},{6,4},{8,10},{10,8},{12,14},{14,12},{16,18},{18,... | collective-permute-start | bytes 3932168 | tf_op jit(solution)/shard_map/ppermute | solution.py:425
  7.9 49.3 %collective-permute-start.5 = (bf16[320,2048]{1,0:T(8,128)(2,1)}, bf16[320,2048]{1,0:T(8,128)(2,1)}, u32[]{:S(2)}, u32[]{:S(2)}) collective-permute-start(bf16[320,2048]{1,0:T(8,128)(2,1)} %get-tuple-element.31.refs_3_.refs_2_), channel_id=1, source_target_pairs={{0,4},{2,6},{4,0},{6,2},{8,12},{10,14},{12,8},{14,10},{16,20},{18,... | collective-permute-start | bytes 3932168 | tf_op jit(solution)/shard_map/ppermute | solution.py:425
  9.3 3.4 %copy-start.1 = (bf16[1,1280,768]{2,1,0:T(8,128)(2,1)S(1)}, bf16[1,1280,768]{2,1,0:T(8,128)(2,1)}, u32[]{:S(2)}) copy-start(bf16[1,1280,768]{2,1,0:T(8,128)(2,1)} %param.7) | copy-start | bytes 5898244
  9.3 1.5 %copy-start.2 = (bf16[320,2048]{1,0:T(8,128)(2,1)S(1)}, bf16[320,2048]{1,0:T(8,128)(2,1)}, u32[]{:S(2)}) copy-start(bf16[320,2048]{1,0:T(8,128)(2,1)} %get-tuple-element.31.refs_3_.refs_2_) | copy-start | bytes 3932164
  10.7 1.0 copy-start.3
  15.3 50.4 %collective-permute-start.6 = (bf16[320,2048]{1,0:T(8,128)(2,1)S(1)}, bf16[320,2048]{1,0:T(8,128)(2,1)S(1)}, u32[]{:S(2)}, u32[]{:S(2)}) collective-permute-start(bf16[320,2048]{1,0:T(8,128)(2,1)S(1)} %forward3.1.refs_2_), channel_id=1, source_target_pairs={{0,6},{2,4},{4,2},{6,0},{8,14},{10,12},{12,10},{14,8},{16,22},{18,... | collective-permute-start | bytes 3932168 | tf_op jit(solution)/shard_map/ppermute | solution.py:425
  15.4 26.4 %collective-permute-start.1 = (bf16[128,2176]{1,0:T(8,128)(2,1)S(1)}, bf16[128,2176]{1,0:T(8,128)(2,1)S(1)}, u32[]{:S(2)}, u32[]{:S(2)}) collective-permute-start(bf16[128,2176]{1,0:T(8,128)(2,1)S(1)} %pack.1.refs_0_.refs_3_), channel_id=1, source_target_pairs={{0,16},{2,18},{4,20},{6,22},{8,24},{10,26},{12,28},{14,30},{16,0},... | collective-permute-start | bytes 1671176 | tf_op jit(solution)/shard_map/ppermute | solution.py:425
  17.9 25.5 %collective-permute-start = (bf16[128,2176]{1,0:T(8,128)(2,1)S(1)}, bf16[128,2176]{1,0:T(8,128)(2,1)S(1)}, u32[]{:S(2)}, u32[]{:S(2)}) collective-permute-start(bf16[128,2176]{1,0:T(8,128)(2,1)S(1)} %pack.1.refs_0_.refs_3_), channel_id=1, source_target_pairs={{0,8},{2,10},{4,12},{6,14},{8,0},{10,2},{12,4},{14,6},{16,24},{18,... | collective-permute-start | bytes 1671176 | tf_op jit(solution)/shard_map/ppermute | solution.py:425
  41.8 13.0 %collective-permute-start.2 = (bf16[128,2176]{1,0:T(8,128)(2,1)S(1)}, bf16[128,2176]{1,0:T(8,128)(2,1)S(1)}, u32[]{:S(2)}, u32[]{:S(2)}) collective-permute-start(bf16[128,2176]{1,0:T(8,128)(2,1)S(1)} %collective-permute-done.1.refs_2_.refs_1_), channel_id=1, source_target_pairs={{0,8},{2,10},{4,12},{6,14},{8,0},{10,2},{12,4},{14,6},{16,24},{18,... | collective-permute-start | bytes 1671176 | tf_op jit(solution)/shard_map/ppermute | solution.py:425
  45.0 3.7 %collective-permute-start.3 = (bf16[320,768]{1,0:T(8,128)(2,1)S(1)}, bf16[320,768]{1,0:T(8,128)(2,1)S(1)}, u32[]{:S(2)}, u32[]{:S(2)}) collective-permute-start(bf16[320,768]{1,0:T(8,128)(2,1)S(1)} %get-tuple-element.33), channel_id=1, source_target_pairs={{0,1},{1,0},{2,3},{3,2},{4,5},{5,4},{6,7},{7,6},{8,9},{9,8},{10,11... | collective-permute-start | bytes 1474568 | tf_op jit(solution)/shard_map/ppermute | solution.py:428
  65.7 22.7 %collective-permute-start.7 = (bf16[528,1024]{1,0:T(8,128)(2,1)S(1)}, bf16[528,1024]{1,0:T(8,128)(2,1)S(1)}, u32[]{:S(2)}, u32[]{:S(2)}) collective-permute-start(bf16[528,1024]{1,0:T(8,128)(2,1)S(1)} %follow.2), channel_id=1, source_target_pairs={{0,2},{2,0},{4,6},{6,4},{8,10},{10,8},{12,14},{14,12},{16,18},{18,... | collective-permute-start | bytes 3244040 | tf_op jit(solution)/shard_map/ppermute | solution.py:425
  66.8 23.3 %collective-permute-start.8 = (bf16[528,1024]{1,0:T(8,128)(2,1)S(1)}, bf16[528,1024]{1,0:T(8,128)(2,1)S(1)}, u32[]{:S(2)}, u32[]{:S(2)}) collective-permute-start(bf16[528,1024]{1,0:T(8,128)(2,1)S(1)} %follow.3), channel_id=1, source_target_pairs={{0,4},{2,6},{4,0},{6,2},{8,12},{10,14},{12,8},{14,10},{16,20},{18,... | collective-permute-start | bytes 3244040 | tf_op jit(solution)/shard_map/ppermute | solution.py:425
  71.2 22.4 %collective-permute-start.11 = (bf16[256,2176]{1,0:T(8,128)(2,1)S(1)}, bf16[256,2176]{1,0:T(8,128)(2,1)S(1)}, u32[]{:S(2)}, u32[]{:S(2)}) collective-permute-start(bf16[256,2176]{1,0:T(8,128)(2,1)S(1)} %combine1.1.refs_2_), channel_id=1, source_target_pairs={{0,8},{2,10},{4,12},{6,14},{8,0},{10,2},{12,4},{14,6},{16,24},{18,... | collective-permute-start | bytes 3342344 | tf_op jit(solution)/shard_map/ppermute | solution.py:425
  72.6 31.6 %collective-permute-start.13 = (bf16[320,1024]{1,0:T(8,128)(2,1)S(1)}, bf16[320,1024]{1,0:T(8,128)(2,1)S(1)}, u32[]{:S(2)}, u32[]{:S(2)}) collective-permute-start(bf16[320,1024]{1,0:T(8,128)(2,1)S(1)} %get-tuple-element.34.refs_2_), channel_id=1, source_target_pairs={{0,2},{2,0},{4,6},{6,4},{8,10},{10,8},{12,14},{14,12},{16,18},{18,... | collective-permute-start | bytes 1966088 | tf_op jit(solution)/shard_map/ppermute | solution.py:425
  75.4 28.8 %collective-permute-start.14 = (bf16[320,1024]{1,0:T(8,128)(2,1)S(1)}, bf16[320,1024]{1,0:T(8,128)(2,1)S(1)}, u32[]{:S(2)}, u32[]{:S(2)}) collective-permute-start(bf16[320,1024]{1,0:T(8,128)(2,1)S(1)} %get-tuple-element.45), channel_id=1, source_target_pairs={{0,4},{2,6},{4,0},{6,2},{8,12},{10,14},{12,8},{14,10},{16,20},{18,... | collective-permute-start | bytes 1966088 | tf_op jit(solution)/shard_map/ppermute | solution.py:425
  91.6 29.6 %collective-permute-start.10 = (bf16[320,1024]{1,0:T(8,128)(2,1)S(1)}, bf16[320,1024]{1,0:T(8,128)(2,1)S(1)}, u32[]{:S(2)}, u32[]{:S(2)}) collective-permute-start(bf16[320,1024]{1,0:T(8,128)(2,1)S(1)} %get-tuple-element.42), channel_id=1, source_target_pairs={{0,2},{2,0},{4,6},{6,4},{8,10},{10,8},{12,14},{14,12},{16,18},{18,... | collective-permute-start | bytes 1966088 | tf_op jit(solution)/shard_map/ppermute | solution.py:425
  92.0 26.2 %collective-permute-start.9 = (bf16[320,1024]{1,0:T(8,128)(2,1)S(1)}, bf16[320,1024]{1,0:T(8,128)(2,1)S(1)}, u32[]{:S(2)}, u32[]{:S(2)}) collective-permute-start(bf16[320,1024]{1,0:T(8,128)(2,1)S(1)} %get-tuple-element.41), channel_id=1, source_target_pairs={{0,4},{2,6},{4,0},{6,2},{8,12},{10,14},{12,8},{14,10},{16,20},{18,... | collective-permute-start | bytes 1966088 | tf_op jit(solution)/shard_map/ppermute | solution.py:425
  93.9 27.3 %collective-permute-start.12 = (bf16[128,2176]{1,0:T(8,128)(2,1)S(1)}, bf16[128,2176]{1,0:T(8,128)(2,1)S(1)}, u32[]{:S(2)}, u32[]{:S(2)}) collective-permute-start(bf16[128,2176]{1,0:T(8,128)(2,1)S(1)} %get-tuple-element.58), channel_id=1, source_target_pairs={{0,16},{2,18},{4,20},{6,22},{8,24},{10,26},{12,28},{14,30},{16,0},... | collective-permute-start | bytes 1671176 | tf_op jit(solution)/shard_map/ppermute | solution.py:425
  112.5 12.8 %collective-permute-start.16 = (bf16[768,1024]{1,0:T(8,128)(2,1)S(1)}, bf16[768,1024]{1,0:T(8,128)(2,1)S(1)}, u32[]{:S(2)}, u32[]{:S(2)}) collective-permute-start(bf16[768,1024]{1,0:T(8,128)(2,1)S(1)} %get-tuple-element.57), channel_id=1, source_target_pairs={{0,1},{1,0},{2,3},{3,2},{4,5},{5,4},{6,7},{7,6},{8,9},{9,8},{10,11... | collective-permute-start | bytes 4718600 | tf_op jit(solution)/shard_map/ppermute | solution.py:428
  118.3 7.1 %collective-permute-start.15 = (bf16[320,1024]{1,0:T(8,128)(2,1)S(1)}, bf16[320,1024]{1,0:T(8,128)(2,1)S(1)}, u32[]{:S(2)}, u32[]{:S(2)}) collective-permute-start(bf16[320,1024]{1,0:T(8,128)(2,1)S(1)} %collective-permute-done.9.refs_0_), channel_id=1, source_target_pairs={{0,1},{1,0},{2,3},{3,2},{4,5},{5,4},{6,7},{7,6},{8,9},{9,8},{10,11... | collective-permute-start | bytes 1966088 | tf_op jit(solution)/shard_map/ppermute | solution.py:428
